TPU v7x, 128 devices: a whole 4x4x4 slice. The times are simulated.
128 devices in a mesh: lat: 16 (over x, y_hi, core), lon: 8 (over y_lo, z).
Axes of the slice: x: 4, y: 4 (y_hi: 2, y_lo: 2; y = y_hi * 2 + y_lo), z: 4, core: 2. Of those that a mesh axis runs over, the one named last changes fastest.
Arguments:
- tokens: bfloat16 [256, 256, 1024], P('lat', 'lon'), may hold values from -6 to 6
- pad_rows: int32 [256], replicated, may hold values from 0 to 1, as said below
- land_sea: int32 [32, 32, 4], P('lat', 'lon'), may hold values from 0 to 1
- win_gain: float32 [1024], replicated, may hold values from 0.5 to 1.5
- win_query: bfloat16 [1024, 1024], replicated, as said below
- win_key: bfloat16 [1024, 1024], replicated, as said below
- win_value: bfloat16 [1024, 1024], replicated, may hold values from -0.1875 to 0.1875
- win_out: bfloat16 [1024, 1024], replicated, may hold values from -0.1875 to 0.1875
- grid_gain: float32 [1024], replicated, may hold values from 0.5 to 1.5
- grid_query: bfloat16 [1024, 1024], replicated, as said below
- grid_key: bfloat16 [1024, 1024], replicated, as said below
- grid_value: bfloat16 [1024, 1024], replicated, may hold values from -0.1875 to 0.1875
- grid_out: bfloat16 [1024, 1024], replicated, may hold values from -0.1875 to 0.1875
Outputs:
- mixed: bfloat16 [256, 256, 1024], P('lat', 'lon')
Inputs may be any that keep to these rules, and one draw needn't show every extreme that they name: pad_rows is 0 on the first 0 to 7 rows and on the final 1 to 7 rows of the grid, and 1 on all others. `win_query`: a projection matrix. `win_key`: a projection matrix. `grid_query`: a projection matrix. `grid_key`: a projection matrix.
All inputs are finite; a program needn't handle non-finite values.
Results may differ from a plain program's by a relative error of at most 0.013.
Values may be sent and summed in bfloat16 or wider, within the bound.
No kernel may reach another device: no remote copies, remote signals or barrier semaphores. Data moves between devices by JAX's collectives and lax.ppermute only.
A program may use at most 128 MiB of HBM per device.

v0:
```python
import math

import jax
import jax.numpy as jnp
from jax import lax
from jax.sharding import PartitionSpec as P

HEADS = 16
GROUPS = 4
WIN = 8
SHIFT = 4


epsilon = 1e-06


def shortened(shard):

    def short(part):
        return part.astype(jnp.bfloat16) if part.dtype == jnp.float32 else part

    return jax.tree.map(short, shard)


def from_behind(block, axis, distance):
    devices = range(lax.axis_size(axis))
    route = [((i - distance) % len(devices), i) for i in devices]
    return lax.ppermute(block, axis, route)


def rms_scale(inputs, gain_row):
    floats = inputs.astype(jnp.float32)
    mean_sq = jnp.mean(floats * floats, axis=-1, keepdims=True)
    return (floats * lax.rsqrt(mean_sq + epsilon) * gain_row).astype(jnp.bfloat16)


def project(inputs, matrix):
    return jnp.dot(inputs, matrix, preferred_element_type=jnp.float32).astype(jnp.bfloat16)


def attend(query_rows, key_rows, value_rows, usable):
    group_count, query_count, features = query_rows.shape
    key_count = key_rows.shape[1]
    head_size = features // HEADS
    query_heads = query_rows.reshape(group_count, query_count, HEADS, head_size)
    key_heads = key_rows.reshape(group_count, key_count, HEADS, head_size)
    value_heads = value_rows.reshape(group_count, key_count, HEADS, head_size)
    scores = jnp.einsum(
        "blhd,bshd->bhls", query_heads, key_heads, preferred_element_type=jnp.float32
    ) * (1.0 / math.sqrt(head_size))
    scores = jnp.where(usable[:, None, None, :], scores, -jnp.inf)
    largest = jnp.max(scores, axis=-1, keepdims=True)
    exponentials = jnp.exp(scores - largest)
    attention = (exponentials / jnp.sum(exponentials, axis=-1, keepdims=True)).astype(jnp.bfloat16)
    return jnp.einsum("bhls,bshd->blhd", attention, value_heads, preferred_element_type=jnp.float32)


def window_mix(normed, pad_band, land_band, query_mat, key_mat, value_mat, out_mat):
    height, breadth, features = normed.shape
    tile_rows = height // WIN
    tile_cols = breadth // WIN
    head_size = features // HEADS
    flat_rows = normed.reshape(height * breadth, features)
    shape_six = (tile_rows, WIN, tile_cols, WIN, HEADS, head_size)
    query_six = project(flat_rows, query_mat).reshape(shape_six)
    key_six = project(flat_rows, key_mat).reshape(shape_six)
    value_six = project(flat_rows, value_mat).reshape(shape_six)
    scores = jnp.einsum(
        "racxhd,rbcyhd->rchaxby", query_six, key_six, preferred_element_type=jnp.float32
    ) * (1.0 / math.sqrt(head_size))
    usable = (pad_band.reshape(tile_rows, WIN) > 0)[:, None, None, None, None, :, None]
    scores = jnp.where(usable, scores, -jnp.inf)
    scores = scores.reshape(tile_rows, tile_cols, HEADS, WIN, WIN, WIN * WIN)
    largest = jnp.max(scores, axis=-1, keepdims=True)
    exponentials = jnp.exp(scores - largest)
    attention = (exponentials / jnp.sum(exponentials, axis=-1, keepdims=True)).astype(jnp.bfloat16)
    attention = attention.reshape(tile_rows, tile_cols, HEADS, WIN, WIN, WIN, WIN)
    heads_out = jnp.einsum(
        "rchaxby,rbcyhd->racxhd", attention, value_six, preferred_element_type=jnp.float32
    )
    head_gate = jnp.repeat(land_band, HEADS // GROUPS, axis=2).astype(jnp.float32)
    heads_out = (heads_out * head_gate[:, None, :, None, :, None]).astype(jnp.bfloat16)
    update = jnp.dot(
        heads_out.reshape(height * breadth, features), out_mat, preferred_element_type=jnp.float32
    )
    return update.reshape(height, breadth, features)


def regroup_out(items, lat_size, lon_size):
    total_cells, row_width = items[0].shape
    portion = total_cells // (lat_size * lon_size)
    shaped = tuple((item.reshape(lat_size * lon_size, portion, 1, row_width) for item in items))
    received = jax.tree.map(
        lambda part, own: part.astype(own.dtype),
        lax.all_to_all(shortened(shaped), ("lat", "lon"), split_axis=0, concat_axis=2, tiled=True),
        shaped,
    )
    return tuple((item.reshape(portion, lat_size * lon_size, row_width) for item in received))


def regroup_back(heads_rows):
    portion, members, row_width = heads_rows.shape
    received = lax.all_to_all(
        heads_rows.reshape(1, portion, members, row_width),
        ("lat", "lon"),
        split_axis=2,
        concat_axis=0,
        tiled=True,
    )
    return received.reshape(members * portion, row_width)


def grid_section(after_window, pad_rows, gain_row, query_mat, key_mat, value_mat, out_mat):
    height, breadth, features = after_window.shape
    total_cells = height * breadth
    lat_size = lax.axis_size("lat")
    lon_size = lax.axis_size("lon")
    members = lat_size * lon_size
    portion = total_cells // members
    normed = rms_scale(after_window, gain_row).reshape(total_cells, features)
    query_rows, key_rows, value_rows = regroup_out(
        (project(normed, query_mat), project(normed, key_mat), project(normed, value_mat)),
        lat_size,
        lon_size,
    )
    flat_index = lax.axis_index("lat") * lon_size + lax.axis_index("lon")
    positions = flat_index * portion + jnp.arange(portion, dtype=jnp.int32)
    local_rows = positions // breadth
    pad_grid = pad_rows.reshape(lat_size, height)
    row_hits = local_rows[:, None, None] == jnp.arange(height, dtype=jnp.int32)[None, None, :]
    pad_lat = jnp.sum(jnp.where(row_hits, pad_grid[None, :, :], 0), axis=2)
    usable = jnp.repeat(pad_lat > 0, lon_size, axis=1)
    heads_out = attend(query_rows, key_rows, value_rows, usable)
    heads_out = heads_out.astype(jnp.bfloat16).reshape(portion, members, features)
    returned = regroup_back(heads_out)
    update = jnp.dot(returned, out_mat, preferred_element_type=jnp.float32).reshape(
        height, breadth, features
    )
    return (after_window.astype(jnp.float32) + update).astype(jnp.bfloat16)


def local(
    tokens,
    pad_rows,
    land_sea,
    win_gain,
    win_query,
    win_key,
    win_value,
    win_out,
    grid_gain,
    grid_query,
    grid_key,
    grid_value,
    grid_out,
):
    height, breadth, features = tokens.shape
    pad_band = lax.dynamic_slice_in_dim(pad_rows, lax.axis_index("lat") * height, height)
    normed = rms_scale(tokens, win_gain)
    edge_cols = from_behind(normed[:, :SHIFT], "lon", -1)
    rolled = jnp.concatenate([normed[:, SHIFT:], edge_cols], axis=1)
    update = window_mix(rolled, pad_band, land_sea, win_query, win_key, win_value, win_out)
    tail_cols = from_behind(update[:, breadth - SHIFT :], "lon", 1)
    restored = jnp.concatenate([tail_cols, update[:, : breadth - SHIFT]], axis=1)
    after_window = (tokens.astype(jnp.float32) + restored).astype(jnp.bfloat16)
    result = grid_section(
        after_window, pad_rows, grid_gain, grid_query, grid_key, grid_value, grid_out
    )
    return result


def solution(mesh):
    placed = (
        P("lat", "lon", None),
        P(),
        P("lat", "lon", None),
        P(),
        P(),
        P(),
        P(),
        P(),
        P(),
        P(),
        P(),
        P(),
        P(),
    )
    return jax.shard_map(
        local, mesh=mesh, in_specs=placed, out_specs=P("lat", "lon", None), check_vma=False
    )
```

profile of v0, /device:TPU:1, one launch (start us, length us, event | category | flops | bytes accessed | tf_op | source)
XLA Modules:
  0.0 215.3 jit_solution(11042152373383757603)
XLA Ops:
  0.0 1.6 fusion.6
  1.7 1.5 fusion.8
  3.3 5.7 %collective-permute-start = (bf16[16,4,1024]{2,1,0:T(4,128)(2,1)S(1)}, bf16[16,4,1024]{2,1,0:T(4,128)(2,1)S(1)}, u32[]{:S(2)}, u32[]{:S(2)}) collective-permute-start(bf16[16,4,1024]{2,1,0:T(4,128)(2,1)S(1)} %slice.17), channel_id=1, source_target_pairs={{1,0},{2,1},{3,2},{4,3},{5,4},{6,5},{7,6},{0,7},{9,8},{10,9},{11,1... | collective-permute-start | bytes 393224 | tf_op jit(solution)/shard_map/ppermute | solution.py:28
  14.9 3.2 %convolution_convert_fusion.3 = bf16[512,1024]{1,0:T(8,128)(2,1)S(1)} fusion(bf16[512,1024]{1,0:T(8,128)(2,1)} %bitcast.83, bf16[1024,1024]{1,0:T(8,128)(2,1)} %param.18), kind=kOutput, calls=%fused_computation.44 | convolution fusion | flops 1074266112 | bytes 4194304 | tf_op jit(solution)/shard_map/dot_general | solution.py:38
  18.1 2.3 %reshape.121 = bf16[2,8,4,8,16,64]{5,4,3,2,1,0:T(8,128)(2,1)} reshape(bf16[512,1024]{1,0:T(8,128)(2,1)S(1)} %convolution_convert_fusion.3) | data formatting | bytes 2097152 | tf_op jit(solution)/shard_map/reshape | solution.py:66
  20.4 3.2 %convolution_convert_fusion.5 = bf16[512,1024]{1,0:T(8,128)(2,1)S(1)} fusion(bf16[512,1024]{1,0:T(8,128)(2,1)} %bitcast.84, bf16[1024,1024]{1,0:T(8,128)(2,1)} %param.19), kind=kOutput, calls=%fused_computation.46 | convolution fusion | flops 1074266112 | bytes 4194304 | tf_op jit(solution)/shard_map/dot_general | solution.py:38
  23.6 2.4 %reshape.119 = bf16[2,8,4,8,16,64]{5,4,3,2,1,0:T(8,128)(2,1)} reshape(bf16[512,1024]{1,0:T(8,128)(2,1)S(1)} %convolution_convert_fusion.5) | data formatting | bytes 2097152 | tf_op jit(solution)/shard_map/reshape | solution.py:67
  25.9 19.7 %fusion.1 = (f32[2,4,16,8,8]{4,3,2,1,0:T(8,128)S(1)}, f32[2,4,16,8,8,8,8]{4,6,5,3,2,1,0:T(8,128)}) fusion(pred[2,8]{1,0:T(4,128)(4,1)S(1)} %gt.17, bf16[2,8,4,8,16,64,1]{5,4,3,2,1,0,6:T(8,128)(2,1)} %bitcast.69, bf16[2,8,4,8,16,64,1]{5,4,3,2,1,0,6:T(8,128)(2,1)S(1)} %bitcast.68), kind=kOutput, calls=%fused_computation.4 | convolution fusion | flops 68673536 | bytes 4227088 | tf_op jit(solution)/shard_map/racxhd,rbcyhd->rchaxby/dot_general | solution.py:68
  45.6 16.7 %fusion.2 = f32[2,4,16,8,8]{4,3,2,1,0:T(8,128)S(1)} fusion(f32[2,4,16,8,8,8,8]{4,6,5,3,2,1,0:T(8,128)} %get-tuple-element.8, f32[2,4,16,8,8]{4,3,2,1,0:T(8,128)S(1)} %get-tuple-element.7, pred[2,8]{1,0:T(4,128)(4,1)S(1)} %gt.17), kind=kLoop, calls=%fused_computation.5 | loop fusion | flops 2088960 | bytes 2162704 | tf_op jit(solution)/shard_map/reduce_sum | solution.py:76
  62.4 13.9 %fusion.26 = bf16[2,8,4,8,16,64]{5,3,1,4,2,0:T(8,128)(2,1)S(1)} fusion(f32[2,4,16]{2,1,0:T(4,128)S(1)} %convert_element_type.75, f32[2,4,16,8,8,8,8]{4,6,5,3,2,1,0:T(8,128)} %get-tuple-element.8, f32[2,4,16,8,8]{4,3,2,1,0:T(8,128)S(1)} %fusion.2, f32[2,4,16,8,8]{4,3,2,1,0:T(8,128)S(1)} %get-tuple-element.7, pred[2,8]{1,0:T(4,128)(4,1)S(1)} %gt.17, ...), kind=kOutput, calls=%fused_computation.39 | convolution fusion | flops 70778880 | bytes 4260368 | tf_op jit(solution)/shard_map/rchaxby,rbcyhd->racxhd/dot_general | solution.py:78
  76.3 2.4 %copy.50 = bf16[2,8,4,8,16,64]{5,4,3,2,1,0:T(8,128)(2,1)S(1)} copy(bf16[2,8,4,8,16,64]{5,3,1,4,2,0:T(8,128)(2,1)S(1)} %fusion.26) | data formatting | bytes 2097152 | tf_op jit(solution)/shard_map/convert_element_type | solution.py:82
  80.3 2.9 %fusion.16 = f32[16,32,1024]{2,1,0:T(8,128)S(1)} fusion(bf16[16,32,1024]{2,1,0:T(8,128)(2,1)S(1)} %dot_general.45, bf16[1024,1024]{1,0:T(8,128)(2,1)} %param.20), kind=kOutput, calls=%fused_computation.29 | convolution fusion | flops 1073741824 | bytes 5242880 | tf_op jit(solution)/shard_map/dot_general | solution.py:83
  83.3 9.4 %collective-permute-done.1 = f32[16,4,1024]{2,1,0:T(4,128)S(1)} collective-permute-done((f32[16,4,1024]{2,1,0:T(4,128)S(1)}, f32[16,4,1024]{2,1,0:T(4,128)S(1)}, u32[]{:S(2)}, u32[]{:S(2)}) %collective-permute-start.1) | collective-permute-done | bytes 262176 | tf_op jit(solution)/shard_map/ppermute | solution.py:28
  93.7 1.6 copy-done.11
  97.8 8.9 %all-to-all-start.1 = ((bf16[128,4,1,1024]{3,1,2,0:T(4,128)(2,1)}), bf16[128,4,1,1024]{3,1,2,0:T(4,128)(2,1)S(1)}, u32[]{:S(2)}, u32[]{:S(2)}) async-start(bf16[128,4,1,1024]{3,1,2,0:T(4,128)(2,1)} %bitcast.14), calls=%async_computation.1 | async-start | bytes 2097152 | tf_op jit(solution)/shard_map/all_to_all | solution.py:95
  106.7 3.8 %convolution_convert_fusion = bf16[512,1024]{1,0:T(8,128)(2,1)} fusion(bf16[512,1024]{1,0:T(8,128)(2,1)S(1)} %bitcast.78, bf16[1024,1024]{1,0:T(8,128)(2,1)} %param.23), kind=kOutput, calls=%fused_computation.41 | convolution fusion | flops 1074266112 | bytes 4194304 | tf_op jit(solution)/shard_map/dot_general | solution.py:38
  110.5 2.2 %reshape.125 = bf16[128,4,1,1024]{3,1,0,2:T(4,128)(2,1)} reshape(bf16[512,1024]{1,0:T(8,128)(2,1)} %convolution_convert_fusion) | data formatting | bytes 2097152 | tf_op jit(solution)/shard_map/reshape | solution.py:92
  112.8 13.3 %all-to-all-done.1 = bf16[128,4,1,1024]{3,1,2,0:T(4,128)(2,1)S(1)} async-done(((bf16[128,4,1,1024]{3,1,2,0:T(4,128)(2,1)}), bf16[128,4,1,1024]{3,1,2,0:T(4,128)(2,1)S(1)}, u32[]{:S(2)}, u32[]{:S(2)}) %all-to-all-start.1) | async-done | bytes 1048608 | tf_op jit(solution)/shard_map/all_to_all | solution.py:95
  126.1 4.2 %all-to-all-start.2 = ((bf16[128,4,1,1024]{3,1,2,0:T(4,128)(2,1)}), bf16[128,4,1,1024]{3,1,2,0:T(4,128)(2,1)S(1)}, u32[]{:S(2)}, u32[]{:S(2)}) async-start(bf16[128,4,1,1024]{3,1,2,0:T(4,128)(2,1)} %bitcast.73), calls=%async_computation.2 | async-start | bytes 2097152 | tf_op jit(solution)/shard_map/all_to_all | solution.py:95
  130.4 4.2 %convolution_convert_fusion.2 = bf16[512,1024]{1,0:T(8,128)(2,1)} fusion(bf16[512,1024]{1,0:T(8,128)(2,1)} %bitcast.79, bf16[1024,1024]{1,0:T(8,128)(2,1)} %param.24), kind=kOutput, calls=%fused_computation.43 | convolution fusion | flops 1074266112 | bytes 4194304 | tf_op jit(solution)/shard_map/dot_general | solution.py:38
  134.6 2.2 %reshape.123 = bf16[128,4,1,1024]{3,1,0,2:T(4,128)(2,1)} reshape(bf16[512,1024]{1,0:T(8,128)(2,1)} %convolution_convert_fusion.2) | data formatting | bytes 2097152 | tf_op jit(solution)/shard_map/reshape | solution.py:92
  136.8 13.1 %all-to-all-done.2 = bf16[128,4,1,1024]{3,1,2,0:T(4,128)(2,1)S(1)} async-done(((bf16[128,4,1,1024]{3,1,2,0:T(4,128)(2,1)}), bf16[128,4,1,1024]{3,1,2,0:T(4,128)(2,1)S(1)}, u32[]{:S(2)}, u32[]{:S(2)}) %all-to-all-start.2) | async-done | bytes 1048608 | tf_op jit(solution)/shard_map/all_to_all | solution.py:95
  149.9 5.3 %all-to-all-start = ((bf16[128,4,1,1024]{3,1,2,0:T(4,128)(2,1)}), bf16[128,4,1,1024]{3,1,2,0:T(4,128)(2,1)}, u32[]{:S(2)}, u32[]{:S(2)}) async-start(bf16[128,4,1,1024]{3,1,2,0:T(4,128)(2,1)} %bitcast.72), calls=%async_computation | async-start | bytes 2097152 | tf_op jit(solution)/shard_map/all_to_all | solution.py:95
  155.7 1.7 copy.54
  157.4 1.7 copy.56
  159.1 15.3 %all-to-all-done = bf16[128,4,1,1024]{3,1,2,0:T(4,128)(2,1)} async-done(((bf16[128,4,1,1024]{3,1,2,0:T(4,128)(2,1)}), bf16[128,4,1,1024]{3,1,2,0:T(4,128)(2,1)}, u32[]{:S(2)}, u32[]{:S(2)}) %all-to-all-start) | async-done | bytes 1048608 | tf_op jit(solution)/shard_map/all_to_all | solution.py:95
  174.4 2.6 %copy.52 = bf16[1,4,128,1,1024]{2,4,1,3,0:T(8,128)(2,1)} copy(bf16[1,4,128,1,1024]{4,1,2,3,0:T(4,128)(2,1)} %bitcast.12) | data formatting | bytes 2097152 | tf_op jit(solution)/shard_map/all_to_all | solution.py:95
  177.1 3.7 %fusion.39 = (f32[4,16,128]{2,1,0:T(8,128)S(1)}, f32[4,16,128,128]{2,3,1,0:T(8,128)}) fusion(pred[4,128]{1,0:T(4,128)(4,1)S(1)} %broadcast_in_dim.74, bf16[4,128,16,64]{1,3,2,0:T(8,128)(2,1)S(1)} %bitcast.80, bf16[4,128,16,64]{1,3,2,0:T(8,128)(2,1)S(1)} %bitcast.81), kind=kOutput, calls=%fused_computation.63 | convolution fusion | flops 138412160 | bytes 6324736 | tf_op jit(solution)/shard_map/sub | solution.py:53
  180.8 3.2 %fusion.29 = bf16[4,16,64,128]{3,2,1,0:T(8,128)(2,1)S(1)} fusion(bf16[4,128,16,64]{1,3,2,0:T(8,128)(2,1)} %bitcast.85, f32[4,16,128,128]{2,3,1,0:T(8,128)} %get-tuple-element.10, f32[4,16,128]{2,1,0:T(8,128)S(1)} %get-tuple-element.9), kind=kOutput, calls=%fused_computation.40 | convolution fusion | flops 136839168 | bytes 6324224 | tf_op jit(solution)/shard_map/bhls,bshd->blhd/dot_general | solution.py:55
  184.9 23.8 %all_to_all.60 = bf16[1,4,128,1024]{3,1,0,2:T(4,128)(2,1)} all-to-all(bf16[1,4,128,1024]{3,1,0,2:T(4,128)(2,1)S(1)} %copy.58), channel_id=1, replica_groups=mesh['lat'=16,'lon'=8] {'lat','lon'}, dimensions={2} | all-to-all | bytes 2097152 | tf_op jit(solution)/shard_map/all_to_all | solution.py:103
  208.8 2.3 %dot_general.52 = bf16[16,32,1024]{2,1,0:T(8,128)(2,1)} reshape(bf16[128,1,4,1,1024]{4,2,0,3,1:T(4,128)(2,1)} %bitcast.74) | data formatting | bytes 2097152 | tf_op jit(solution)/shard_map/dot_general | solution.py:136
  211.1 4.1 %fusion.13 = bf16[16,32,1024]{2,1,0:T(8,128)(2,1)} fusion(bf16[16,32,1024]{2,1,0:T(8,128)(2,1)S(1)} %get-tuple-element.6, bf16[16,32,1024]{2,1,0:T(8,128)(2,1)} %dot_general.52, bf16[1024,1024]{1,0:T(8,128)(2,1)} %param.25), kind=kOutput, calls=%fused_computation.26 | convolution fusion | flops 1075314688 | bytes 5242880 | tf_op jit(solution)/shard_map/dot_general | solution.py:136
  (51 shorter events, 12.5 us)
Async XLA Ops:
  0.0 12.3 %copy-start = (bf16[1024,1024]{1,0:T(8,128)(2,1)S(1)}, bf16[1024,1024]{1,0:T(8,128)(2,1)}, u32[]{:S(2)}) copy-start(bf16[1024,1024]{1,0:T(8,128)(2,1)} %param.17) | copy-start | bytes 6291460
  1.7 7.7 %copy-start.10 = (s32[256]{0:T(256)S(1)}, s32[256]{0:T(256)}, u32[]{:S(2)}) copy-start(s32[256]{0:T(256)} %param.14) | copy-start | bytes 3076
  1.7 7.8 %copy-start.9 = (s32[2,4,4]{2,1,0:T(4,128)S(1)}, s32[2,4,4]{2,1,0:T(4,128)}, u32[]{:S(2)}) copy-start(s32[2,4,4]{2,1,0:T(4,128)} %param.15) | copy-start | bytes 388
  3.3 7.8 %collective-permute-start = (bf16[16,4,1024]{2,1,0:T(4,128)(2,1)S(1)}, bf16[16,4,1024]{2,1,0:T(4,128)(2,1)S(1)}, u32[]{:S(2)}, u32[]{:S(2)}) collective-permute-start(bf16[16,4,1024]{2,1,0:T(4,128)(2,1)S(1)} %slice.17), channel_id=1, source_target_pairs={{1,0},{2,1},{3,2},{4,3},{5,4},{6,5},{7,6},{0,7},{9,8},{10,9},{11,1... | collective-permute-start | bytes 393224 | tf_op jit(solution)/shard_map/ppermute | solution.py:28
  11.3 1.0 copy-start.7
  45.6 16.8 %copy-start.3 = (bf16[2,8,4,8,16,64]{5,4,3,2,1,0:T(8,128)(2,1)S(1)}, bf16[2,8,4,8,16,64]{5,4,3,2,1,0:T(8,128)(2,1)}, u32[]{:S(2)}) copy-start(bf16[2,8,4,8,16,64]{5,4,3,2,1,0:T(8,128)(2,1)} %reshape.119) | copy-start | bytes 3145732
  80.2 12.5 %copy-start.2 = (bf16[16,32,1024]{2,1,0:T(8,128)(2,1)S(1)}, bf16[16,32,1024]{2,1,0:T(8,128)(2,1)}, u32[]{:S(2)}) copy-start(bf16[16,32,1024]{2,1,0:T(8,128)(2,1)} %param.13) | copy-start | bytes 3145732
  83.3 9.5 %collective-permute-start.1 = (f32[16,4,1024]{2,1,0:T(4,128)S(1)}, f32[16,4,1024]{2,1,0:T(4,128)S(1)}, u32[]{:S(2)}, u32[]{:S(2)}) collective-permute-start(f32[16,4,1024]{2,1,0:T(4,128)S(1)} %slice.18), channel_id=1, source_target_pairs={{7,0},{0,1},{1,2},{2,3},{3,4},{4,5},{5,6},{6,7},{15,8},{8,9},{9,10... | collective-permute-start | bytes 786440 | tf_op jit(solution)/shard_map/ppermute | solution.py:28
  92.7 0.7 copy-start.8
  93.3 2.0 copy-start.11
  93.7 13.0 %copy-start.4 = (bf16[16,32,1024]{2,1,0:T(8,128)(2,1)}, bf16[16,32,1024]{2,1,0:T(8,128)(2,1)S(1)}, u32[]{:S(2)}) copy-start(bf16[16,32,1024]{2,1,0:T(8,128)(2,1)S(1)} %fusion.12) | copy-start | bytes 3145732
  97.8 28.3 %all-to-all-start.1 = ((bf16[128,4,1,1024]{3,1,2,0:T(4,128)(2,1)}), bf16[128,4,1,1024]{3,1,2,0:T(4,128)(2,1)S(1)}, u32[]{:S(2)}, u32[]{:S(2)}) async-start(bf16[128,4,1,1024]{3,1,2,0:T(4,128)(2,1)} %bitcast.14), calls=%async_computation.1 | async-start | bytes 2097152 | tf_op jit(solution)/shard_map/all_to_all | solution.py:95
  126.1 23.8 %all-to-all-start.2 = ((bf16[128,4,1,1024]{3,1,2,0:T(4,128)(2,1)}), bf16[128,4,1,1024]{3,1,2,0:T(4,128)(2,1)S(1)}, u32[]{:S(2)}, u32[]{:S(2)}) async-start(bf16[128,4,1,1024]{3,1,2,0:T(4,128)(2,1)} %bitcast.73), calls=%async_computation.2 | async-start | bytes 2097152 | tf_op jit(solution)/shard_map/all_to_all | solution.py:95
  149.9 24.5 %all-to-all-start = ((bf16[128,4,1,1024]{3,1,2,0:T(4,128)(2,1)}), bf16[128,4,1,1024]{3,1,2,0:T(4,128)(2,1)}, u32[]{:S(2)}, u32[]{:S(2)}) async-start(bf16[128,4,1,1024]{3,1,2,0:T(4,128)(2,1)} %bitcast.72), calls=%async_computation | async-start | bytes 2097152 | tf_op jit(solution)/shard_map/all_to_all | solution.py:95
  157.4 19.7 %copy-start.5 = (bf16[1,4,128,1,1024]{2,4,1,3,0:T(8,128)(2,1)S(1)}, bf16[1,4,128,1,1024]{2,4,1,3,0:T(8,128)(2,1)}, u32[]{:S(2)}) copy-start(bf16[1,4,128,1,1024]{2,4,1,3,0:T(8,128)(2,1)} %copy.54) | copy-start | bytes 3145732
  159.1 18.0 %copy-start.6 = (bf16[1,4,128,1,1024]{2,4,1,3,0:T(8,128)(2,1)S(1)}, bf16[1,4,128,1,1024]{2,4,1,3,0:T(8,128)(2,1)}, u32[]{:S(2)}) copy-start(bf16[1,4,128,1,1024]{2,4,1,3,0:T(8,128)(2,1)} %copy.56) | copy-start | bytes 3145732
  208.8 6.5 %copy-start.1 = (bf16[1024,1024]{1,0:T(8,128)(2,1)S(1)}, bf16[1024,1024]{1,0:T(8,128)(2,1)}, u32[]{:S(2)}) copy-start(bf16[1024,1024]{1,0:T(8,128)(2,1)} %param.17) | copy-start | bytes 6291460
where the time goes:
time: 216 us; the launch traced here: 215 us
  matrix products  64.5 us (30%)
  waiting for transfers between devices  52.6 us (24%)
  local copies, waits for them, and re-layouts  28.5 us (13%)
  starting transfers between devices  24.2 us (11%)
  blocking collectives  23.8 us (11%)
  other arithmetic  21.4 us (10%)
    all_to_all x3, waiting for transfers between devices, regroup_out(): lax.all_to_all(shortened(shaped), ('lat', 'lon'), split_axis=0, concat_ax...  41.8 us
    all_to_all x1, blocking collectives, regroup_back(): lax.all_to_all(heads_rows.reshape(1, portion, members, row_width), ('lat'...  23.8 us
    dot_general x1, matrix products, window_mix(): jnp.einsum('racxhd,rbcyhd->rchaxby', query_six, key_six, preferred_elemen...  19.7 us
    all_to_all x3, starting transfers between devices, regroup_out(): lax.all_to_all(shortened(shaped), ('lat', 'lon'), split_axis=0, concat_ax...  18.4 us
    dot_general x6, matrix products, project(): jnp.dot(inputs, matrix, preferred_element_type=jnp.float32)  16.9 us
    reduce_sum x1, other arithmetic, window_mix(): jnp.sum(exponentials, axis=-1, keepdims=True)  16.7 us
    dot_general x1, matrix products, window_mix(): jnp.einsum('rchaxby,rbcyhd->racxhd', attention, value_six, preferred_elem...  13.9 us
    ppermute x2, waiting for transfers between devices, from_behind(): return lax.ppermute(block, axis, route)  10.8 us
  transfers between devices with their start and end apart: 5, of which 5 were waited for; matrix products, arithmetic and copies ran while one was open for 8% of the time, Pallas kernels for 0%

commit v1 on v0

v1 whole, which is shorter than its diff:
```python
import functools
import math

import jax
import jax.numpy as jnp
from jax import lax
from jax.experimental import pallas as pl
from jax.experimental.pallas import tpu as pltpu
from jax.sharding import PartitionSpec as P

HEADS = 16
GROUPS = 4
WIN = 8
SHIFT = 4
EPSILON = 1e-06
MASKED = -1e30
BF16 = jnp.bfloat16
F32 = jnp.float32
I32 = jnp.int32


def iota(shape, axis):
    return lax.broadcasted_iota(I32, shape, axis)


def one_hot(hits):
    return jnp.where(hits, 1.0, 0.0).astype(BF16)


def matmul(left, right):
    return jnp.dot(left, right, preferred_element_type=F32)


def matmul_nt(left, right):
    return lax.dot_general(left, right, (((1,), (1,)), ((), ())), preferred_element_type=F32)


def norm(rows, gain):
    mean_sq = jnp.mean(rows * rows, axis=-1, keepdims=True)
    return (rows * lax.rsqrt(mean_sq + EPSILON) * gain).astype(BF16)


def usable_bias(pad_ref, wanted_row):
    lanes = wanted_row.shape[1]
    pads = jnp.broadcast_to(pad_ref[...].astype(F32).astype(BF16), (16, pad_ref.shape[1]))
    picks = one_hot(iota((pad_ref.shape[1], lanes), 0) == wanted_row)
    return jnp.where(matmul(pads, picks)[:1] > 0.5, 0.0, MASKED)


def tile_place(part, row):
    if part == 0:
        tile = row // 64
        return (tile // 2) * 8 + (row // 8) % 8, (tile % 2) * 8 + row % 8
    half = row - 128
    whole_row, whole_col = (row // 64) * 8 + (row // 8) % 8, row % 8
    half_row, half_col = (half % 64) // 4, 8 + (half // 64) * 4 + half % 4
    whole = row < 128
    return jnp.where(whole, whole_row, half_row), jnp.where(whole, whole_col, half_col)


def window_kernel(part, *refs):
    if part == 0:
        tok_ref, pad_ref, land_ref, gain_ref, *refs = refs
    else:
        tok_ref, right_ref, left_ref, pad_ref, land_ref, land_left_ref, gain_ref, *refs = refs
    wq_hbm, wk_hbm, wv_hbm, wo_hbm, out_ref, weights, q_ref, k_ref, v_ref, heads_ref, sems = refs
    copies = [
        pltpu.make_async_copy(source, weights.at[n], sems.at[n])
        for n, source in enumerate((wq_hbm, wk_hbm, wv_hbm, wo_hbm))
    ]
    for copy in copies:
        copy.start()
    cells, width = tok_ref.shape
    rows = cells // 2
    row, col = tile_place(part, iota((rows, 1), 0))
    source = row * 32 + (4 + 16 * part + col) % 32
    order = one_hot(iota((rows, cells), 1) == source)
    x = matmul(order, tok_ref[...])
    gain = gain_ref[...]
    normed = norm(x, gain)
    if part == 1:
        halo = jnp.concatenate([right_ref[...], left_ref[...]], axis=0).astype(F32)
        all_normed = jnp.concatenate([normed, norm(halo, gain)], axis=0)
    else:
        all_normed = normed
    head_size = width // HEADS
    copies[0].wait()
    factor = math.log2(math.e) / math.sqrt(head_size)
    q_ref[...] = (matmul(normed, weights[0]) * factor).astype(BF16)
    copies[1].wait()
    k_ref[...] = matmul(all_normed, weights[1]).astype(BF16)
    copies[2].wait()
    v_ref[...] = matmul(all_normed, weights[2]).astype(BF16)

    quad = 4 * head_size
    first = lax.axis_index("lat") * 16
    key_lane = iota((1, quad), 1) % 64
    biases = {}
    for tile_row in range(2):
        biases[tile_row, True] = usable_bias(pad_ref, first + tile_row * 8 + key_lane // 8)
        if part == 1:
            biases[tile_row, False] = usable_bias(
                pad_ref, first + tile_row * 8 + (key_lane % 32) // 4
            )
    head_lane = iota((1, quad), 1) // head_size
    masks = [one_hot(head_lane == h) for h in range(4)]
    ones = one_hot(iota((quad, quad), 0) // 64 == iota((quad, quad), 1) // head_size)
    lower = iota((1, 128), 1) < 64

    def spread(block):
        return jnp.concatenate([block * mask for mask in masks], axis=0)

    tiles = []
    if part == 0:
        for tile_row in range(2):
            for tile_col in range(2):
                start = (tile_row * 2 + tile_col) * 64
                tiles.append((start, 64, ((start, 64),), tile_row, True, (land_ref, tile_col)))
    else:
        for tile_row in range(2):
            start = tile_row * 64
            tiles.append((start, 64, ((start, 64),), tile_row, True, (land_ref, 2)))
        for side in range(2):
            for tile_row in range(2):
                start = 128 + (side * 2 + tile_row) * 32
                spans = ((start, 32), (start + 128, 32))
                gates = (land_ref, 3) if side == 0 else (land_left_ref, 0)
                tiles.append((start, 32, spans, tile_row, False, gates))
    for start, count, spans, tile_row, whole, (gate_ref, tile_col) in tiles:
        for group in range(GROUPS):
            lanes = slice(group * quad, (group + 1) * quad)
            query = q_ref[start : start + count, lanes]
            key = jnp.concatenate([k_ref[s : s + n, lanes] for s, n in spans], axis=0)
            value = jnp.concatenate([v_ref[s : s + n, lanes] for s, n in spans], axis=0)
            scores = matmul_nt(query, spread(key)) + biases[tile_row, whole]
            exps = []
            for block in range(2):
                part_scores = scores[:, block * 128 : (block + 1) * 128]
                low = jnp.max(jnp.where(lower, part_scores, -jnp.inf), axis=1, keepdims=True)
                high = jnp.max(jnp.where(lower, -jnp.inf, part_scores), axis=1, keepdims=True)
                exps.append(jnp.exp2(part_scores - jnp.where(lower, low, high)).astype(BF16))
            weight = jnp.concatenate(exps, axis=1)
            total = matmul(weight, ones)
            gate = gate_ref[tile_row, tile_col, group].astype(F32)
            heads = matmul(weight, spread(value)) / total * gate
            heads_ref[start : start + count, lanes] = heads.astype(BF16)
    copies[3].wait()
    after = (x + matmul(heads_ref[...], weights[3])).astype(BF16)
    row, col = tile_place(part, iota((1, rows), 1))
    back = one_hot(iota((rows, rows), 0) == row * 16 + col)
    out_ref[...] = matmul(back, after).astype(BF16)


def window_part(part, tokens, halos, pads, land_sea, land_left, gain, weights):
    cells, width = tokens.shape
    rows = cells // 2
    key_rows = rows if part == 0 else rows + 128
    vmem = pl.BlockSpec(memory_space=pltpu.VMEM)
    smem = pl.BlockSpec(memory_space=pltpu.SMEM)
    hbm = pl.BlockSpec(memory_space=pl.ANY)
    if part == 0:
        args, specs = (tokens, pads, land_sea, gain), [vmem, vmem, smem, vmem]
    else:
        args = (tokens, *halos, pads, land_sea, land_left, gain)
        specs = [vmem, vmem, vmem, vmem, smem, smem, vmem]
    return pl.pallas_call(
        functools.partial(window_kernel, part),
        out_shape=jax.ShapeDtypeStruct((rows, width), BF16),
        in_specs=specs + [hbm] * 4,
        out_specs=vmem,
        scratch_shapes=[
            pltpu.VMEM((4, width, width), BF16),
            pltpu.VMEM((rows, width), BF16),
            pltpu.VMEM((key_rows, width), BF16),
            pltpu.VMEM((key_rows, width), BF16),
            pltpu.VMEM((rows, width), BF16),
            pltpu.SemaphoreType.DMA((4,)),
        ],
        compiler_params=pltpu.CompilerParams(vmem_limit_bytes=40 * 2**20),
        cost_estimate=pl.CostEstimate(
            flops=8 * rows * width * width, bytes_accessed=12 * 2**20, transcendentals=rows * 1024
        ),
        name=f"window_part{part}",
    )(*args, *weights)


def grid_kernel(cell_ref, pad_ref, gain_ref, *refs):
    wq_hbm, wk_hbm, wv_hbm, wo_hbm, out_ref, weights, q_ref, k_ref, v_ref, heads_ref, sems = refs
    copies = [
        pltpu.make_async_copy(source, weights.at[n], sems.at[n])
        for n, source in enumerate((wq_hbm, wk_hbm, wv_hbm, wo_hbm))
    ]
    for copy in copies:
        copy.start()
    rows, width = cell_ref.shape
    members = 128
    groups = rows // members
    row = iota((rows, 1), 0)
    order = one_hot(iota((rows, rows), 1) == (row % members) * groups + row // members)
    x = matmul(order, cell_ref[...])
    normed = norm(x, gain_ref[...])
    head_size = width // HEADS
    copies[0].wait()
    factor = math.log2(math.e) / math.sqrt(head_size)
    q_ref[...] = (matmul(normed, weights[0]) * factor).astype(BF16)
    copies[1].wait()
    k_ref[...] = matmul(normed, weights[1]).astype(BF16)
    copies[2].wait()
    v_ref[...] = matmul(normed, weights[2]).astype(BF16)

    pair = 2 * head_size
    key_lane = iota((1, 2 * members), 1) % members
    bias = usable_bias(pad_ref, (key_lane // 8) * 16 + lax.axis_index("lat"))
    masks = [one_hot(iota((1, pair), 1) // head_size == h) for h in range(2)]
    ones = one_hot(
        iota((2 * members, pair), 0) // members == iota((2 * members, pair), 1) // head_size
    )

    def spread(block):
        return jnp.concatenate([block * mask for mask in masks], axis=0)

    for group in range(groups):
        span = slice(group * members, (group + 1) * members)
        for two in range(HEADS // 2):
            lanes = slice(two * pair, (two + 1) * pair)
            scores = matmul_nt(q_ref[span, lanes], spread(k_ref[span, lanes])) + bias
            exps = []
            for half in range(2):
                head_scores = scores[:, half * members : (half + 1) * members]
                largest = jnp.max(head_scores, axis=1, keepdims=True)
                exps.append(jnp.exp2(head_scores - largest).astype(BF16))
            weight = jnp.concatenate(exps, axis=1)
            both = jnp.concatenate([spread(v_ref[span, lanes]), ones], axis=1)
            sums = matmul(weight, both)
            heads_ref[span, lanes] = (sums[:, :pair] / sums[:, pair:]).astype(BF16)
    copies[3].wait()
    mixed = (x + matmul(heads_ref[...], weights[3])).astype(BF16)
    col = iota((1, rows), 1)
    back = one_hot(iota((rows, rows), 0) == (col % members) * groups + col // members)
    out_ref[...] = matmul(back, mixed).astype(BF16)


def grid_part(cells, pads, gain, weights):
    rows, width = cells.shape
    vmem = pl.BlockSpec(memory_space=pltpu.VMEM)
    hbm = pl.BlockSpec(memory_space=pl.ANY)
    return pl.pallas_call(
        grid_kernel,
        out_shape=jax.ShapeDtypeStruct((rows, width), BF16),
        in_specs=[vmem] * 3 + [hbm] * 4,
        out_specs=vmem,
        scratch_shapes=[
            pltpu.VMEM((4, width, width), BF16),
            pltpu.VMEM((rows, width), BF16),
            pltpu.VMEM((rows, width), BF16),
            pltpu.VMEM((rows, width), BF16),
            pltpu.VMEM((rows, width), BF16),
            pltpu.SemaphoreType.DMA((4,)),
        ],
        compiler_params=pltpu.CompilerParams(vmem_limit_bytes=40 * 2**20),
        cost_estimate=pl.CostEstimate(
            flops=8 * rows * width * width, bytes_accessed=10 * 2**20, transcendentals=rows * 2048
        ),
        name="grid_part",
    )(cells, pads, gain, *weights)


def from_behind(block, axis, distance):
    devices = range(lax.axis_size(axis))
    route = [((i - distance) % len(devices), i) for i in devices]
    return lax.ppermute(block, axis, route)


def exchange(rows):
    count, width = rows.shape
    members = lax.axis_size("lat") * lax.axis_size("lon")
    blocks = rows.reshape(members, count // members, width)
    moved = lax.all_to_all(blocks, ("lat", "lon"), split_axis=0, concat_axis=0, tiled=True)
    return moved.reshape(count, width)


def local(
    tokens,
    pad_rows,
    land_sea,
    win_gain,
    win_query,
    win_key,
    win_value,
    win_out,
    grid_gain,
    grid_query,
    grid_key,
    grid_value,
    grid_out,
):
    height, breadth, width = tokens.shape
    flat = tokens.reshape(height * breadth, width)
    pads = pad_rows.reshape(1, -1)
    right = from_behind(tokens[:, :SHIFT], "lon", -1).reshape(height * SHIFT, width)
    left = from_behind(tokens[:, breadth - SHIFT :], "lon", 1).reshape(height * SHIFT, width)
    land_left = from_behind(land_sea[:, -1:], "lon", 1)
    win_weights = (win_query, win_key, win_value, win_out)
    grid_weights = (grid_query, grid_key, grid_value, grid_out)
    results = []
    for part in range(2):
        after = window_part(
            part,
            flat,
            (right, left),
            pads,
            land_sea,
            land_left,
            win_gain.reshape(1, -1),
            win_weights,
        )
        cells = exchange(after)
        mixed = grid_part(cells, pads, grid_gain.reshape(1, -1), grid_weights)
        results.append(exchange(mixed).reshape(height, breadth // 2, width))
    inner, outer = results
    return jnp.concatenate([outer[:, 12:], inner, outer[:, :12]], axis=1)


def solution(mesh):
    whole = P()
    split = P("lat", "lon", None)
    placed = (split, whole, split) + (whole,) * 10
    return jax.shard_map(local, mesh=mesh, in_specs=placed, out_specs=split, check_vma=False)
```

time: 216 us -> 127 us (0.59)
  matrix products: 64.5 us -> 0 us
  waiting for transfers between devices: 52.6 us -> 23.3 us
  blocking collectives: 23.8 us -> 0 us
  Pallas kernels: 0 us -> 23.7 us
  other arithmetic: 21.4 us -> 1.41 us
  starting transfers between devices: 24.2 us -> 40.1 us
  local copies, waits for them, and re-layouts: 28.5 us -> 37.3 us
    dot_general x11 -> x0, matrix products: 60.8 us -> none  [the longest x1 19.7 us: window_mix(): jnp.einsum('racxhd,rbcyhd->rchaxby', query_six, key_six, preferred_elemen...]
    all_to_all x3 -> x4, waiting for transfers between devices: 41.8 us -> 16.1 us  [exchange(): lax.all_to_all(blocks, ('lat', 'lon'), split_axis=0, concat_axis=0, tiled...]
    all_to_all x1 -> x0, blocking collectives: 23.8 us -> none  [regroup_back(): lax.all_to_all(heads_rows.reshape(1, portion, members, row_width), ('lat'...]
    pallas_call x0 -> x4, Pallas kernels: none -> 23.7 us  [the longest x2 13.8 us: window_part(): pl.pallas_call(functools.partial(window_kernel, part), out_shape=jax.Shap...]
    unnamed x24 -> x52, local copies, waits for them, and re-layouts: 2.65 us -> 25.5 us
    reduce_sum x4 -> x0, other arithmetic: 19.1 us -> none  [the longest x1 16.7 us: window_mix(): jnp.sum(exponentials, axis=-1, keepdims=True)]
    all_to_all x3 -> x4, starting transfers between devices: 18.4 us -> 35.8 us  [exchange(): lax.all_to_all(blocks, ('lat', 'lon'), split_axis=0, concat_axis=0, tiled...]
    all_to_all x3 -> x0, local copies, waits for them, and re-layouts: 6.01 us -> none  [regroup_out(): lax.all_to_all(shortened(shaped), ('lat', 'lon'), split_axis=0, concat_ax...]
  transfers between devices with their start and end apart: 5 -> 7, of which waited for: 5 -> 4; matrix products, arithmetic and copies ran while one was open for 8% -> 7% of each run, Pallas kernels for 0% -> 14%
where the time goes in v1:
time: 127 us; the launch traced here: 126 us
  starting transfers between devices  40.1 us (32%)
  local copies, waits for them, and re-layouts  37.3 us (29%)
  Pallas kernels  23.7 us (19%)
  waiting for transfers between devices  23.3 us (18%)
  other arithmetic  1.41 us (1%)
    all_to_all x4, starting transfers between devices, exchange(): lax.all_to_all(blocks, ('lat', 'lon'), split_axis=0, concat_axis=0, tiled...  35.8 us
    unnamed x52, local copies, waits for them, and re-layouts  25.5 us
    all_to_all x4, waiting for transfers between devices, exchange(): lax.all_to_all(blocks, ('lat', 'lon'), split_axis=0, concat_axis=0, tiled...  16.1 us
    pallas_call x2, Pallas kernels, window_part(): pl.pallas_call(functools.partial(window_kernel, part), out_shape=jax.Shap...  13.8 us
    pallas_call x2, Pallas kernels, grid_part(): pl.pallas_call(grid_kernel, out_shape=jax.ShapeDtypeStruct((rows, width),...  9.83 us
    ppermute x3, waiting for transfers between devices, from_behind(): return lax.ppermute(block, axis, route)  7.24 us
    reshape x4, local copies, waits for them, and re-layouts, exchange(): blocks = rows.reshape(members, count // members, width)  6.36 us
    ppermute x3, starting transfers between devices, from_behind(): return lax.ppermute(block, axis, route)  4.23 us
  transfers between devices with their start and end apart: 7, of which 4 were waited for; matrix products, arithmetic and copies ran while one was open for 7% of the time, Pallas kernels for 14%

profile of v1, /device:TPU:1, one launch (start us, length us, event | category | flops | bytes accessed | tf_op | source)
XLA Modules:
  0.0 126.0 jit_solution(15935474492249155491)
XLA Ops:
  0.0 1.6 %copy-done = bf16[1024,1024]{1,0:T(8,128)(2,1)S(1)} copy-done((bf16[1024,1024]{1,0:T(8,128)(2,1)S(1)}, bf16[1024,1024]{1,0:T(8,128)(2,1)}, u32[]{:S(2)}) %copy-start) | copy-done | bytes 2097176
  1.6 1.6 %copy-done.2 = bf16[1024,1024]{1,0:T(8,128)(2,1)S(1)} copy-done((bf16[1024,1024]{1,0:T(8,128)(2,1)S(1)}, bf16[1024,1024]{1,0:T(8,128)(2,1)}, u32[]{:S(2)}) %copy-start.2) | copy-done | bytes 2097176
  3.2 1.6 %copy-done.4 = bf16[1024,1024]{1,0:T(8,128)(2,1)S(1)} copy-done((bf16[1024,1024]{1,0:T(8,128)(2,1)S(1)}, bf16[1024,1024]{1,0:T(8,128)(2,1)}, u32[]{:S(2)}) %copy-start.4) | copy-done | bytes 2097176
  4.8 1.6 %copy-done.6 = bf16[1024,1024]{1,0:T(8,128)(2,1)S(1)} copy-done((bf16[1024,1024]{1,0:T(8,128)(2,1)S(1)}, bf16[1024,1024]{1,0:T(8,128)(2,1)}, u32[]{:S(2)}) %copy-start.6) | copy-done | bytes 2097176
  9.6 6.3 %window_part0.1 = bf16[256,1024]{1,0:T(8,128)(2,1)S(1)} custom-call(bf16[512,1024]{1,0:T(8,128)(2,1)S(1)} %bitcast.5, s32[1,256]{1,0:T(1,128)S(1)} %bitcast.11, s32[2,4,4]{2,1,0:T(4,128)S(1)} %copy-done.19, f32[1,1024]{1,0:T(1,128)S(1)} %bitcast.7, bf16[1024,1024]{1,0:T(8,128)(2,1)S(1)} %copy-done, bf16[1024,1024]{1,0:T(8,128)(2,1)S(1)} %copy-done.2, ...), custom_call_target="tpu_custom_call" | custom-call | flops 2147483648 | bytes 12582912 | tf_op jit(solution)/shard_map/window_part0/pallas_call | solution.py:166
  16.8 2.2 %reshape.47 = bf16[128,2,1024]{2,1,0:T(2,128)(2,1)} reshape(bf16[256,1024]{1,0:T(8,128)(2,1)} %copy-done.18) | data formatting | bytes 1048576 | tf_op jit(solution)/shard_map/reshape | solution.py:277
  19.0 12.0 %all-to-all-start.2 = ((bf16[128,2,1024]{2,1,0:T(2,128)(2,1)}), bf16[128,2,1024]{2,1,0:T(2,128)(2,1)}, u32[]{:S(2)}, u32[]{:S(2)}) async-start(bf16[128,2,1024]{2,1,0:T(2,128)(2,1)} %reshape.47), calls=%async_computation.2 | async-start | bytes 1048576 | tf_op jit(solution)/shard_map/all_to_all | solution.py:278
  31.7 1.5 %collective-permute-start.1 = (bf16[16,4,1024]{2,1,0:T(4,128)(2,1)S(1)}, bf16[16,4,1024]{2,1,0:T(4,128)(2,1)S(1)}, u32[]{:S(2)}, u32[]{:S(2)}) collective-permute-start(bf16[16,4,1024]{2,1,0:T(4,128)(2,1)S(1)} %get-tuple-element.5), channel_id=1, source_target_pairs={{7,0},{0,1},{1,2},{2,3},{3,4},{4,5},{5,6},{6,7},{15,8},{8,9},{9,10... | collective-permute-start | bytes 393224 | tf_op jit(solution)/shard_map/ppermute | solution.py:271
  33.2 2.7 %collective-permute-start = (bf16[16,4,1024]{2,1,0:T(4,128)(2,1)}, bf16[16,4,1024]{2,1,0:T(4,128)(2,1)S(1)}, u32[]{:S(2)}, u32[]{:S(2)}) collective-permute-start(bf16[16,4,1024]{2,1,0:T(4,128)(2,1)} %get-tuple-element.6), channel_id=1, source_target_pairs={{1,0},{2,1},{3,2},{4,3},{5,4},{6,5},{7,6},{0,7},{9,8},{10,9},{11,1... | collective-permute-start | bytes 393224 | tf_op jit(solution)/shard_map/ppermute | solution.py:271
  36.5 7.2 %collective-permute-done.1 = bf16[16,4,1024]{2,1,0:T(4,128)(2,1)S(1)} collective-permute-done((bf16[16,4,1024]{2,1,0:T(4,128)(2,1)S(1)}, bf16[16,4,1024]{2,1,0:T(4,128)(2,1)S(1)}, u32[]{:S(2)}, u32[]{:S(2)}) %collective-permute-start.1) | collective-permute-done | bytes 131104 | tf_op jit(solution)/shard_map/ppermute | solution.py:271
  43.9 1.6 %copy-done.3 = bf16[1024,1024]{1,0:T(8,128)(2,1)S(1)} copy-done((bf16[1024,1024]{1,0:T(8,128)(2,1)S(1)}, bf16[1024,1024]{1,0:T(8,128)(2,1)}, u32[]{:S(2)}) %copy-start.3) | copy-done | bytes 2097176
  45.5 1.6 %copy-done.5 = bf16[1024,1024]{1,0:T(8,128)(2,1)S(1)} copy-done((bf16[1024,1024]{1,0:T(8,128)(2,1)S(1)}, bf16[1024,1024]{1,0:T(8,128)(2,1)}, u32[]{:S(2)}) %copy-start.5) | copy-done | bytes 2097176
  47.1 1.6 %copy-done.7 = bf16[1024,1024]{1,0:T(8,128)(2,1)S(1)} copy-done((bf16[1024,1024]{1,0:T(8,128)(2,1)S(1)}, bf16[1024,1024]{1,0:T(8,128)(2,1)}, u32[]{:S(2)}) %copy-start.7) | copy-done | bytes 2097176
  48.7 7.5 %window_part1.1 = bf16[256,1024]{1,0:T(8,128)(2,1)S(1)} custom-call(bf16[512,1024]{1,0:T(8,128)(2,1)S(1)} %bitcast.6, bf16[64,1024]{1,0:T(8,128)(2,1)S(1)} %reshape.39.refs_1_, bf16[64,1024]{1,0:T(8,128)(2,1)S(1)} %reshape.40.refs_2_, s32[1,256]{1,0:T(1,128)S(1)} %bitcast.12, s32[2,4,4]{2,1,0:T(4,128)S(1)} %copy-done.20, ...), custom_call_target="tpu_custom_call" | custom-call | flops 2147483648 | bytes 12582912 | tf_op jit(solution)/shard_map/window_part1/pallas_call | solution.py:166
  57.0 2.2 %reshape.43 = bf16[128,2,1024]{2,1,0:T(2,128)(2,1)} reshape(bf16[256,1024]{1,0:T(8,128)(2,1)} %copy-done.17) | data formatting | bytes 1048576 | tf_op jit(solution)/shard_map/reshape | solution.py:277
  59.2 7.2 %all-to-all-start = ((bf16[128,2,1024]{2,1,0:T(2,128)(2,1)}), bf16[128,2,1024]{2,1,0:T(2,128)(2,1)}, u32[]{:S(2)}, u32[]{:S(2)}) async-start(bf16[128,2,1024]{2,1,0:T(2,128)(2,1)} %reshape.43), calls=%async_computation | async-start | bytes 1048576 | tf_op jit(solution)/shard_map/all_to_all | solution.py:278
  66.4 1.2 reshape.48.cell_ref
  67.7 1.6 %copy-done.9 = bf16[1024,1024]{1,0:T(8,128)(2,1)S(1)} copy-done((bf16[1024,1024]{1,0:T(8,128)(2,1)S(1)}, bf16[1024,1024]{1,0:T(8,128)(2,1)}, u32[]{:S(2)}) %copy-start.9) | copy-done | bytes 2097176
  69.3 1.6 %copy-done.11 = bf16[1024,1024]{1,0:T(8,128)(2,1)S(1)} copy-done((bf16[1024,1024]{1,0:T(8,128)(2,1)S(1)}, bf16[1024,1024]{1,0:T(8,128)(2,1)}, u32[]{:S(2)}) %copy-start.11) | copy-done | bytes 2097176
  70.9 1.6 %copy-done.13 = bf16[1024,1024]{1,0:T(8,128)(2,1)S(1)} copy-done((bf16[1024,1024]{1,0:T(8,128)(2,1)S(1)}, bf16[1024,1024]{1,0:T(8,128)(2,1)}, u32[]{:S(2)}) %copy-start.13) | copy-done | bytes 2097176
  72.5 4.9 %grid_part.3 = bf16[256,1024]{1,0:T(8,128)(2,1)S(1)} custom-call(bf16[256,1024]{1,0:T(8,128)(2,1)S(1)} %reshape.48.cell_ref, s32[1,256]{1,0:T(1,128)S(1)} %bitcast.13, f32[1,1024]{1,0:T(1,128)S(1)} %bitcast.9, bf16[1024,1024]{1,0:T(8,128)(2,1)S(1)} %copy-done.8, bf16[1024,1024]{1,0:T(8,128)(2,1)S(1)} %copy-done.9, bf16[1024,1024]{1,0:T(8,128)(2,1)S(1)} %copy-done.11, ...), custom_call_target="tpu_custom_call" | custom-call | flops 2147483648 | bytes 10485760 | tf_op jit(solution)/shard_map/grid_part/pallas_call | solution.py:247
  78.4 1.7 %all-to-all-done = bf16[128,2,1024]{2,1,0:T(2,128)(2,1)} async-done(((bf16[128,2,1024]{2,1,0:T(2,128)(2,1)}), bf16[128,2,1024]{2,1,0:T(2,128)(2,1)}, u32[]{:S(2)}, u32[]{:S(2)}) %all-to-all-start) | async-done | bytes 524320 | tf_op jit(solution)/shard_map/all_to_all | solution.py:278
  80.0 8.5 %all-to-all-start.3 = ((bf16[128,2,1024]{2,1,0:T(2,128)(2,1)}), bf16[128,2,1024]{2,1,0:T(2,128)(2,1)}, u32[]{:S(2)}, u32[]{:S(2)}) async-start(bf16[128,2,1024]{2,1,0:T(2,128)(2,1)} %reshape.49), calls=%async_computation.3 | async-start | bytes 1048576 | tf_op jit(solution)/shard_map/all_to_all | solution.py:278
  88.6 1.2 reshape.44.cell_ref
  89.9 1.6 %copy-done.10 = bf16[1024,1024]{1,0:T(8,128)(2,1)S(1)} copy-done((bf16[1024,1024]{1,0:T(8,128)(2,1)S(1)}, bf16[1024,1024]{1,0:T(8,128)(2,1)}, u32[]{:S(2)}) %copy-start.10) | copy-done | bytes 2097176
  91.4 1.6 %copy-done.12 = bf16[1024,1024]{1,0:T(8,128)(2,1)S(1)} copy-done((bf16[1024,1024]{1,0:T(8,128)(2,1)S(1)}, bf16[1024,1024]{1,0:T(8,128)(2,1)}, u32[]{:S(2)}) %copy-start.12) | copy-done | bytes 2097176
  93.0 1.6 %copy-done.14 = bf16[1024,1024]{1,0:T(8,128)(2,1)S(1)} copy-done((bf16[1024,1024]{1,0:T(8,128)(2,1)S(1)}, bf16[1024,1024]{1,0:T(8,128)(2,1)}, u32[]{:S(2)}) %copy-start.14) | copy-done | bytes 2097176
  94.6 4.9 %grid_part.2 = bf16[256,1024]{1,0:T(8,128)(2,1)S(1)} custom-call(bf16[256,1024]{1,0:T(8,128)(2,1)S(1)} %reshape.44.cell_ref, s32[1,256]{1,0:T(1,128)S(1)} %bitcast.14, f32[1,1024]{1,0:T(1,128)S(1)} %bitcast.10, bf16[1024,1024]{1,0:T(8,128)(2,1)S(1)} %copy-done.8, bf16[1024,1024]{1,0:T(8,128)(2,1)S(1)} %copy-done.10, bf16[1024,1024]{1,0:T(8,128)(2,1)S(1)} %copy-done.12, ...), custom_call_target="tpu_custom_call" | custom-call | flops 2147483648 | bytes 10485760 | tf_op jit(solution)/shard_map/grid_part/pallas_call | solution.py:247
  100.5 1.7 %all-to-all-done.3 = bf16[128,2,1024]{2,1,0:T(2,128)(2,1)} async-done(((bf16[128,2,1024]{2,1,0:T(2,128)(2,1)}), bf16[128,2,1024]{2,1,0:T(2,128)(2,1)}, u32[]{:S(2)}, u32[]{:S(2)}) %all-to-all-start.3) | async-done | bytes 524320 | tf_op jit(solution)/shard_map/all_to_all | solution.py:278
  102.2 8.1 %all-to-all-start.1 = ((bf16[128,2,1024]{2,1,0:T(2,128)(2,1)}), bf16[128,2,1024]{2,1,0:T(2,128)(2,1)S(1)}, u32[]{:S(2)}, u32[]{:S(2)}) async-start(bf16[128,2,1024]{2,1,0:T(2,128)(2,1)} %reshape.46), calls=%async_computation.1 | async-start | bytes 1048576 | tf_op jit(solution)/shard_map/all_to_all | solution.py:278
  111.6 12.7 %all-to-all-done.1 = bf16[128,2,1024]{2,1,0:T(2,128)(2,1)S(1)} async-done(((bf16[128,2,1024]{2,1,0:T(2,128)(2,1)}), bf16[128,2,1024]{2,1,0:T(2,128)(2,1)S(1)}, u32[]{:S(2)}, u32[]{:S(2)}) %all-to-all-start.1) | async-done | bytes 524320 | tf_op jit(solution)/shard_map/all_to_all | solution.py:278
  124.6 1.4 %pad_maximum_fusion = bf16[16,32,1024]{2,1,0:T(8,128)(2,1)} fusion(bf16[16,12,1024]{2,1,0:T(8,128)(2,1)S(1)} %bitcast.15, bf16[16,16,1024]{2,1,0:T(8,128)(2,1)S(1)} %reshape_reshape.7, bf16[16,4,1024]{2,1,0:T(4,128)(2,1)S(1)} %slice.20), kind=kLoop, calls=%fused_computation | loop fusion | flops 3145728 | bytes 2097152 | tf_op jit(solution)/shard_map/concatenate | solution.py:321
  (52 shorter events, 9.8 us)
Async XLA Ops:
  0.0 1.6 %copy-start = (bf16[1024,1024]{1,0:T(8,128)(2,1)S(1)}, bf16[1024,1024]{1,0:T(8,128)(2,1)}, u32[]{:S(2)}) copy-start(bf16[1024,1024]{1,0:T(8,128)(2,1)} %refs_4_.3) | copy-start | bytes 6291460
  1.6 1.6 %copy-start.2 = (bf16[1024,1024]{1,0:T(8,128)(2,1)S(1)}, bf16[1024,1024]{1,0:T(8,128)(2,1)}, u32[]{:S(2)}) copy-start(bf16[1024,1024]{1,0:T(8,128)(2,1)} %refs_5_.1) | copy-start | bytes 6291460
  3.2 1.6 %copy-start.4 = (bf16[1024,1024]{1,0:T(8,128)(2,1)S(1)}, bf16[1024,1024]{1,0:T(8,128)(2,1)}, u32[]{:S(2)}) copy-start(bf16[1024,1024]{1,0:T(8,128)(2,1)} %refs_6_.1) | copy-start | bytes 6291460
  4.8 1.6 %copy-start.6 = (bf16[1024,1024]{1,0:T(8,128)(2,1)S(1)}, bf16[1024,1024]{1,0:T(8,128)(2,1)}, u32[]{:S(2)}) copy-start(bf16[1024,1024]{1,0:T(8,128)(2,1)} %refs_7_.3) | copy-start | bytes 6291460
  6.4 1.2 copy-start.15
  7.6 0.7 copy-start.19
  8.3 0.7 copy-start.21
  9.6 21.3 %copy-start.16 = (bf16[16,32,1024]{2,1,0:T(8,128)(2,1)S(1)}, bf16[16,32,1024]{2,1,0:T(8,128)(2,1)}, u32[]{:S(2)}) copy-start(bf16[16,32,1024]{2,1,0:T(8,128)(2,1)} %param.13) | copy-start | bytes 3145732
  16.0 0.8 copy-start.18
  16.8 19.2 %copy-start.20 = (s32[2,4,4]{2,1,0:T(4,128)S(1)}, s32[2,4,4]{2,1,0:T(4,128)}, u32[]{:S(2)}) copy-start(s32[2,4,4]{2,1,0:T(4,128)} %refs_2_.4) | copy-start | bytes 388
  16.8 27.1 %copy-start.1 = (bf16[1024,1024]{1,0:T(8,128)(2,1)S(1)}, bf16[1024,1024]{1,0:T(8,128)(2,1)}, u32[]{:S(2)}) copy-start(bf16[1024,1024]{1,0:T(8,128)(2,1)} %refs_4_.3) | copy-start | bytes 6291460
  16.8 27.1 %copy-start.22 = (f32[1024]{0:T(1024)S(1)}, f32[1024]{0:T(1024)}, u32[]{:S(2)}) copy-start(f32[1024]{0:T(1024)} %param.16) | copy-start | bytes 12292
  16.8 27.1 %copy-start.25 = (s32[256]{0:T(256)S(1)}, s32[256]{0:T(256)}, u32[]{:S(2)}) copy-start(s32[256]{0:T(256)} %param.14) | copy-start | bytes 3076
  19.0 40.2 %all-to-all-start.2 = ((bf16[128,2,1024]{2,1,0:T(2,128)(2,1)}), bf16[128,2,1024]{2,1,0:T(2,128)(2,1)}, u32[]{:S(2)}, u32[]{:S(2)}) async-start(bf16[128,2,1024]{2,1,0:T(2,128)(2,1)} %reshape.47), calls=%async_computation.2 | async-start | bytes 1048576 | tf_op jit(solution)/shard_map/all_to_all | solution.py:278
  31.7 12.0 %collective-permute-start.1 = (bf16[16,4,1024]{2,1,0:T(4,128)(2,1)S(1)}, bf16[16,4,1024]{2,1,0:T(4,128)(2,1)S(1)}, u32[]{:S(2)}, u32[]{:S(2)}) collective-permute-start(bf16[16,4,1024]{2,1,0:T(4,128)(2,1)S(1)} %get-tuple-element.5), channel_id=1, source_target_pairs={{7,0},{0,1},{1,2},{2,3},{3,4},{4,5},{5,6},{6,7},{15,8},{8,9},{9,10... | collective-permute-start | bytes 393224 | tf_op jit(solution)/shard_map/ppermute | solution.py:271
  33.2 10.6 %collective-permute-start = (bf16[16,4,1024]{2,1,0:T(4,128)(2,1)}, bf16[16,4,1024]{2,1,0:T(4,128)(2,1)S(1)}, u32[]{:S(2)}, u32[]{:S(2)}) collective-permute-start(bf16[16,4,1024]{2,1,0:T(4,128)(2,1)} %get-tuple-element.6), channel_id=1, source_target_pairs={{1,0},{2,1},{3,2},{4,3},{5,4},{6,5},{7,6},{0,7},{9,8},{10,9},{11,1... | collective-permute-start | bytes 393224 | tf_op jit(solution)/shard_map/ppermute | solution.py:271
  36.5 7.3 %collective-permute-start.2 = (s32[2,1,4]{2,1,0:T(1,128)}, s32[2,1,4]{2,1,0:T(1,128)S(1)}, u32[]{:S(2)}, u32[]{:S(2)}) collective-permute-start(s32[2,1,4]{2,1,0:T(1,128)} %slice.17), channel_id=1, source_target_pairs={{7,0},{0,1},{1,2},{2,3},{3,4},{4,5},{5,6},{6,7},{15,8},{8,9},{9,10... | collective-permute-start | bytes 104 | tf_op jit(solution)/shard_map/ppermute | solution.py:271
  43.9 1.6 %copy-start.3 = (bf16[1024,1024]{1,0:T(8,128)(2,1)S(1)}, bf16[1024,1024]{1,0:T(8,128)(2,1)}, u32[]{:S(2)}) copy-start(bf16[1024,1024]{1,0:T(8,128)(2,1)} %refs_5_.1) | copy-start | bytes 6291460
  45.5 1.6 %copy-start.5 = (bf16[1024,1024]{1,0:T(8,128)(2,1)S(1)}, bf16[1024,1024]{1,0:T(8,128)(2,1)}, u32[]{:S(2)}) copy-start(bf16[1024,1024]{1,0:T(8,128)(2,1)} %refs_6_.1) | copy-start | bytes 6291460
  47.1 1.6 %copy-start.7 = (bf16[1024,1024]{1,0:T(8,128)(2,1)S(1)}, bf16[1024,1024]{1,0:T(8,128)(2,1)}, u32[]{:S(2)}) copy-start(bf16[1024,1024]{1,0:T(8,128)(2,1)} %refs_7_.3) | copy-start | bytes 6291460
  56.2 0.8 copy-start.17
  57.0 10.7 %copy-start.8 = (bf16[1024,1024]{1,0:T(8,128)(2,1)S(1)}, bf16[1024,1024]{1,0:T(8,128)(2,1)}, u32[]{:S(2)}) copy-start(bf16[1024,1024]{1,0:T(8,128)(2,1)} %refs_0_.3) | copy-start | bytes 6291460
  57.0 10.7 %copy-start.23 = (f32[1024]{0:T(1024)S(1)}, f32[1024]{0:T(1024)}, u32[]{:S(2)}) copy-start(f32[1024]{0:T(1024)} %param.21) | copy-start | bytes 12292
  59.2 20.9 %all-to-all-start = ((bf16[128,2,1024]{2,1,0:T(2,128)(2,1)}), bf16[128,2,1024]{2,1,0:T(2,128)(2,1)}, u32[]{:S(2)}, u32[]{:S(2)}) async-start(bf16[128,2,1024]{2,1,0:T(2,128)(2,1)} %reshape.43), calls=%async_computation | async-start | bytes 1048576 | tf_op jit(solution)/shard_map/all_to_all | solution.py:278
  67.7 1.6 %copy-start.9 = (bf16[1024,1024]{1,0:T(8,128)(2,1)S(1)}, bf16[1024,1024]{1,0:T(8,128)(2,1)}, u32[]{:S(2)}) copy-start(bf16[1024,1024]{1,0:T(8,128)(2,1)} %refs_1_.3) | copy-start | bytes 6291460
  69.3 1.6 %copy-start.11 = (bf16[1024,1024]{1,0:T(8,128)(2,1)S(1)}, bf16[1024,1024]{1,0:T(8,128)(2,1)}, u32[]{:S(2)}) copy-start(bf16[1024,1024]{1,0:T(8,128)(2,1)} %refs_2_.5) | copy-start | bytes 6291460
  70.9 1.6 %copy-start.13 = (bf16[1024,1024]{1,0:T(8,128)(2,1)S(1)}, bf16[1024,1024]{1,0:T(8,128)(2,1)}, u32[]{:S(2)}) copy-start(bf16[1024,1024]{1,0:T(8,128)(2,1)} %refs_3_.3) | copy-start | bytes 6291460
  80.0 22.2 %all-to-all-start.3 = ((bf16[128,2,1024]{2,1,0:T(2,128)(2,1)}), bf16[128,2,1024]{2,1,0:T(2,128)(2,1)}, u32[]{:S(2)}, u32[]{:S(2)}) async-start(bf16[128,2,1024]{2,1,0:T(2,128)(2,1)} %reshape.49), calls=%async_computation.3 | async-start | bytes 1048576 | tf_op jit(solution)/shard_map/all_to_all | solution.py:278
  89.8 1.6 %copy-start.10 = (bf16[1024,1024]{1,0:T(8,128)(2,1)S(1)}, bf16[1024,1024]{1,0:T(8,128)(2,1)}, u32[]{:S(2)}) copy-start(bf16[1024,1024]{1,0:T(8,128)(2,1)} %refs_1_.3) | copy-start | bytes 6291460
  91.4 1.6 %copy-start.12 = (bf16[1024,1024]{1,0:T(8,128)(2,1)S(1)}, bf16[1024,1024]{1,0:T(8,128)(2,1)}, u32[]{:S(2)}) copy-start(bf16[1024,1024]{1,0:T(8,128)(2,1)} %refs_2_.5) | copy-start | bytes 6291460
  93.0 1.6 %copy-start.14 = (bf16[1024,1024]{1,0:T(8,128)(2,1)S(1)}, bf16[1024,1024]{1,0:T(8,128)(2,1)}, u32[]{:S(2)}) copy-start(bf16[1024,1024]{1,0:T(8,128)(2,1)} %refs_3_.3) | copy-start | bytes 6291460
  102.2 22.1 %all-to-all-start.1 = ((bf16[128,2,1024]{2,1,0:T(2,128)(2,1)}), bf16[128,2,1024]{2,1,0:T(2,128)(2,1)S(1)}, u32[]{:S(2)}, u32[]{:S(2)}) async-start(bf16[128,2,1024]{2,1,0:T(2,128)(2,1)} %reshape.46), calls=%async_computation.1 | async-start | bytes 1048576 | tf_op jit(solution)/shard_map/all_to_all | solution.py:278
  (1 other events, 0.7 us)

commit v2 on v1

v2 whole, which is shorter than its diff:
```python
import functools
import math

import jax
import jax.numpy as jnp
from jax import lax
from jax.experimental import pallas as pl
from jax.experimental.pallas import tpu as pltpu
from jax.sharding import PartitionSpec as P

HEADS = 16
GROUPS = 4
WIN = 8
SHIFT = 4
EPSILON = 1e-06
MASKED = -1e30
BF16 = jnp.bfloat16
F32 = jnp.float32
I32 = jnp.int32


def iota(shape, axis):
    return lax.broadcasted_iota(I32, shape, axis)


def one_hot(hits):
    return jnp.where(hits, 1.0, 0.0).astype(BF16)


def matmul(left, right):
    return jnp.dot(left, right, preferred_element_type=F32)


def matmul_nt(left, right):
    return lax.dot_general(left, right, (((1,), (1,)), ((), ())), preferred_element_type=F32)


def norm(rows, gain):
    mean_sq = jnp.mean(rows * rows, axis=-1, keepdims=True)
    return (rows * lax.rsqrt(mean_sq + EPSILON) * gain).astype(BF16)


def usable_bias(pad_ref, wanted_row):
    lanes = wanted_row.shape[1]
    pads = jnp.broadcast_to(pad_ref[...].astype(F32).astype(BF16), (16, pad_ref.shape[1]))
    picks = one_hot(iota((pad_ref.shape[1], lanes), 0) == wanted_row)
    return jnp.where(matmul(pads, picks)[:1] > 0.5, 0.0, MASKED)


def fetch(pairs, sems):
    copies = [
        pltpu.make_async_copy(source, target, sems.at[n]) for n, (source, target) in enumerate(pairs)
    ]
    for copy in copies:
        copy.start()
    return copies


def cross(upper, lower):
    first = iota((1, 8, 1), 1) < 4
    return (
        jnp.where(first, upper, jnp.roll(lower, 4, axis=1)),
        jnp.where(first, jnp.roll(upper, 4, axis=1), lower),
    )


def to_blocks(rows):
    count, width = rows.shape
    half = width // 2
    tiles = rows.reshape(count // 8, 8, width)
    even, odd = cross(tiles[:, :, :half], tiles[:, :, half:])
    return jnp.stack([even, odd], axis=1).reshape(2 * count, half)


def from_blocks(blocks):
    count, half = blocks.shape
    tiles = blocks.reshape(count // 16, 2, 8, half)
    first, second = cross(tiles[:, 0], tiles[:, 1])
    return jnp.concatenate([first, second], axis=2).reshape(count // 2, 2 * half)


def project(rows, weight, target_ref, factor=None):
    product = matmul(rows, weight[...])
    if factor is not None:
        product = product * factor
    target_ref[...] = product.astype(BF16)


def query_factor(head_size):
    return math.log2(math.e) / math.sqrt(head_size)


def window_attention(tiles, pad_ref, land_ref, q_ref, k_ref, v_ref, heads_ref):
    width = q_ref.shape[1]
    head_size = width // HEADS
    quad = 4 * head_size
    first = lax.axis_index("lat") * 16
    key_lane = iota((1, quad), 1) % 64
    biases = [usable_bias(pad_ref, first + band * 8 + key_lane // 8) for band in range(2)]
    head_lane = iota((1, quad), 1) // head_size
    masks = [one_hot(head_lane == h) for h in range(4)]
    ones = one_hot(iota((quad, quad), 0) // 64 == iota((quad, quad), 1) // head_size)
    lower = iota((1, 128), 1) < 64

    def spread(block):
        return jnp.concatenate([block * mask for mask in masks], axis=0)

    for tile, (band, tile_col) in enumerate(tiles):
        span = slice(tile * 64, (tile + 1) * 64)
        for group in range(GROUPS):
            lanes = slice(group * quad, (group + 1) * quad)
            scores = matmul_nt(q_ref[span, lanes], spread(k_ref[span, lanes])) + biases[band]
            exps = []
            for block in range(2):
                part_scores = scores[:, block * 128 : (block + 1) * 128]
                low = jnp.max(jnp.where(lower, part_scores, -jnp.inf), axis=1, keepdims=True)
                high = jnp.max(jnp.where(lower, -jnp.inf, part_scores), axis=1, keepdims=True)
                exps.append(jnp.exp2(part_scores - jnp.where(lower, low, high)).astype(BF16))
            weight = jnp.concatenate(exps, axis=1)
            total = matmul(weight, ones)
            gate = land_ref[band, tile_col, group].astype(F32)
            heads = matmul(weight, spread(v_ref[span, lanes])) / total * gate
            heads_ref[span, lanes] = heads.astype(BF16)


def inner_kernel(
    tok_hbm, pad_hbm, land_hbm, gain_hbm, wq_hbm, wk_hbm, wv_hbm, wo_hbm,
    out_ref, wq_ref, wk_ref, wv_ref, wo_ref,
    tok_ref, pad_ref, land_ref, gain_ref, q_ref, k_ref, v_ref, heads_ref, sems,
):
    copies = fetch(
        [
            (tok_hbm, tok_ref), (gain_hbm, gain_ref), (pad_hbm, pad_ref), (land_hbm, land_ref),
            (wq_hbm, wq_ref), (wk_hbm, wk_ref), (wv_hbm, wv_ref), (wo_hbm, wo_ref),
        ],
        sems,
    )
    cells, width = tok_ref.shape
    rows = heads_ref.shape[0]
    row = iota((rows, 1), 0)
    tile, line, col = row // 64, (row // 8) % 8, row % 8
    source = ((tile // 3) * 8 + line) * 32 + SHIFT + (tile % 3) * 8 + col
    order = one_hot(iota((rows, cells), 1) == source)
    for copy in copies[:4]:
        copy.wait()
    x = matmul(order, tok_ref[...])
    normed = norm(x, gain_ref[...])
    copies[4].wait()
    project(normed, wq_ref, q_ref, query_factor(width // HEADS))
    copies[5].wait()
    project(normed, wk_ref, k_ref)
    copies[6].wait()
    project(normed, wv_ref, v_ref)
    tiles = [(band, tile_col) for band in range(2) for tile_col in range(3)]
    window_attention(tiles, pad_ref, land_ref, q_ref, k_ref, v_ref, heads_ref)
    copies[7].wait()
    out_ref[...] = (x + matmul(heads_ref[...], wo_ref[...])).astype(BF16)


def outer_kernel(
    after_ref, halo_ref, wq_ref, wk_ref, wv_ref, wo_ref,
    tok_hbm, pad_hbm, land_hbm, gain_hbm, gq_hbm, gk_hbm, gv_hbm, go_hbm,
    out_ref, gq_ref, gk_ref, gv_ref, go_ref,
    tok_ref, pad_ref, land_ref, gain_ref, q_ref, k_ref, v_ref, heads_ref, sems,
):
    copies = fetch(
        [
            (tok_hbm, tok_ref), (gain_hbm, gain_ref), (pad_hbm, pad_ref), (land_hbm, land_ref),
            (gq_hbm, gq_ref), (gk_hbm, gk_ref), (gv_hbm, gv_ref), (go_hbm, go_ref),
        ],
        sems,
    )
    cells, width = tok_ref.shape
    halo_rows = halo_ref.shape[0]
    rows = heads_ref.shape[0]
    row = iota((rows, 1), 0)
    line, col = row // 8, row % 8
    own = one_hot(iota((rows, cells), 1) == jnp.where(col < 4, line * 32 + 28 + col, -1))
    halo = one_hot(iota((rows, halo_rows), 1) == jnp.where(col < 4, -1, line * SHIFT + col - 4))
    for copy in copies[:4]:
        copy.wait()
    x = matmul(own, tok_ref[...]) + matmul(halo, halo_ref[...])
    normed = norm(x, gain_ref[...])
    project(normed, wq_ref, q_ref, query_factor(width // HEADS))
    project(normed, wk_ref, k_ref)
    project(normed, wv_ref, v_ref)
    tiles = [(band, 3) for band in range(2)]
    window_attention(tiles, pad_ref, land_ref, q_ref, k_ref, v_ref, heads_ref)
    after = (x + matmul(heads_ref[...], wo_ref[...])).astype(BF16)
    inner_rows = after_ref.shape[0]
    row = iota((1, inner_rows), 1)
    tile, line, col = row // 64, (row // 8) % 8, row % 8
    place = ((tile // 3) * 8 + line) * 32 + SHIFT + (tile % 3) * 8 + col
    inner = one_hot(iota((cells, inner_rows), 0) == place)
    row = iota((1, rows), 1)
    outer = one_hot(iota((cells, rows), 0) == (row // 8) * 32 + (28 + row % 8) % 32)
    both = matmul(inner, after_ref[...]) + matmul(outer, after)
    out_ref[...] = to_blocks(both).astype(BF16)
    for copy in copies[4:]:
        copy.wait()


def in_hbm(arrays):
    return [pltpu.with_memory_space_constraint(a, pltpu.HBM) for a in arrays]


VMEM_SPEC = pl.BlockSpec(memory_space=pltpu.VMEM)
HBM_SPEC = pl.BlockSpec(memory_space=pltpu.HBM)


def call(kernel, name, outs, in_vmem, from_hbm, scratch, rows, exps):
    width = 1024
    return pl.pallas_call(
        kernel,
        out_shape=outs,
        in_specs=[VMEM_SPEC] * len(in_vmem) + [HBM_SPEC] * len(from_hbm),
        out_specs=[VMEM_SPEC] * len(outs),
        scratch_shapes=scratch,
        compiler_params=pltpu.CompilerParams(vmem_limit_bytes=28 * 2**20),
        cost_estimate=pl.CostEstimate(
            flops=8 * rows * width * width, bytes_accessed=10 * 2**20, transcendentals=exps
        ),
        name=name,
    )(*in_vmem, *in_hbm(from_hbm))


def window_part(tokens, halo, pads, land_sea, gain, weights, grid_weights):
    cells, width = tokens.shape
    held = [pltpu.VMEM((width, width), BF16)] * 4
    small = [
        pltpu.VMEM((cells, width), BF16),
        pltpu.VMEM(pads.shape, I32),
        pltpu.SMEM(land_sea.shape, I32),
        pltpu.VMEM(gain.shape, F32),
    ]
    inner, outer = cells * 3 // 4, cells // 4
    sems = pltpu.SemaphoreType.DMA((8,))
    after, *window_weights = call(
        inner_kernel,
        "window_inner",
        [pltpu.VMEM((inner, width), BF16)] + held,
        [],
        [tokens, pads, land_sea, gain, *weights],
        small + [pltpu.VMEM((inner, width), BF16)] * 4 + [sems],
        inner,
        inner * 1024,
    )
    return call(
        outer_kernel,
        "window_outer",
        [jax.ShapeDtypeStruct((2 * cells, width // 2), BF16)] + held,
        [after, halo, *window_weights],
        [tokens, pads, land_sea, gain, *grid_weights],
        small + [pltpu.VMEM((outer, width), BF16)] * 4 + [sems],
        outer,
        outer * 1024,
    )


def grid_kernel(
    block_ref, wq_ref, wk_ref, wv_ref, wo_ref, pad_hbm, gain_hbm,
    out_ref, pad_ref, gain_ref, q_ref, k_ref, v_ref, heads_ref, sems,
):
    copies = fetch([(gain_hbm, gain_ref), (pad_hbm, pad_ref)], sems)
    rows, width = q_ref.shape
    members = 128
    groups = rows // members
    head_size = width // HEADS
    pair = 2 * head_size
    cells = from_blocks(block_ref[...].astype(F32)).astype(BF16)
    row = iota((rows, 1), 0)
    order = one_hot(iota((rows, rows), 1) == (row % members) * groups + row // members)
    x = matmul(order, cells)
    for copy in copies:
        copy.wait()
    normed = norm(x, gain_ref[...])
    project(normed, wq_ref, q_ref, query_factor(head_size))
    project(normed, wk_ref, k_ref)
    project(normed, wv_ref, v_ref)
    key_lane = iota((1, 2 * members), 1) % members
    bias = usable_bias(pad_ref, (key_lane // 8) * 16 + lax.axis_index("lat"))
    masks = [one_hot(iota((1, pair), 1) // head_size == h) for h in range(2)]
    ones = one_hot(
        iota((2 * members, pair), 0) // members == iota((2 * members, pair), 1) // head_size
    )

    def spread(block):
        return jnp.concatenate([block * mask for mask in masks], axis=0)

    for group in range(groups):
        span = slice(group * members, (group + 1) * members)
        for two in range(HEADS // 2):
            lanes = slice(two * pair, (two + 1) * pair)
            scores = matmul_nt(q_ref[span, lanes], spread(k_ref[span, lanes])) + bias
            exps = []
            for half in range(2):
                head_scores = scores[:, half * members : (half + 1) * members]
                largest = jnp.max(head_scores, axis=1, keepdims=True)
                exps.append(jnp.exp2(head_scores - largest).astype(BF16))
            weight = jnp.concatenate(exps, axis=1)
            both = jnp.concatenate([spread(v_ref[span, lanes]), ones], axis=1)
            sums = matmul(weight, both)
            heads_ref[span, lanes] = (sums[:, :pair] / sums[:, pair:]).astype(BF16)
    mixed = (x + matmul(heads_ref[...], wo_ref[...])).astype(BF16)
    col = iota((1, rows), 1)
    member, group = col % members, col // members
    wrapped = jnp.where(lax.axis_index("lon") == 0, 1, 0)
    home = (member // 8) * 8 + (member + wrapped) % 8
    back = one_hot(iota((rows, rows), 0) == home * groups + group)
    out_ref[...] = to_blocks(matmul(back, mixed)).astype(BF16)


def grid_part(blocks, pads, gain, weights):
    rows, width = blocks.shape[0] // 2, blocks.shape[1] * 2
    return call(
        grid_kernel,
        "grid_part",
        [jax.ShapeDtypeStruct(blocks.shape, BF16)],
        [blocks, *weights],
        [pads, gain],
        [pltpu.VMEM(pads.shape, I32), pltpu.VMEM(gain.shape, F32)]
        + [pltpu.VMEM((rows, width), BF16)] * 4
        + [pltpu.SemaphoreType.DMA((2,))],
        rows,
        rows * 2048,
    )[0]


def from_behind(block, axis, distance):
    devices = range(lax.axis_size(axis))
    route = [((i - distance) % len(devices), i) for i in devices]
    return lax.ppermute(block, axis, route)


def exchange(blocks):
    count, width = blocks.shape
    members = lax.axis_size("lat") * lax.axis_size("lon")
    split = blocks.reshape(members, count // members, width)
    moved = lax.all_to_all(split, ("lat", "lon"), split_axis=0, concat_axis=0, tiled=True)
    return moved.reshape(count, width)


def local(
    tokens,
    pad_rows,
    land_sea,
    win_gain,
    win_query,
    win_key,
    win_value,
    win_out,
    grid_gain,
    grid_query,
    grid_key,
    grid_value,
    grid_out,
):
    height, breadth, width = tokens.shape
    flat = tokens.reshape(height * breadth, width)
    pads = pad_rows.reshape(1, -1)
    halo = from_behind(tokens[:, :SHIFT].reshape(height * SHIFT, width), "lon", -1)
    win_weights = (win_query, win_key, win_value, win_out)
    grid_weights = (grid_query, grid_key, grid_value, grid_out)
    blocks, *held = window_part(
        flat, halo, pads, land_sea, win_gain.reshape(1, -1), win_weights, grid_weights
    )
    mixed = exchange(grid_part(exchange(blocks), pads, grid_gain.reshape(1, -1), held))
    halves = mixed.reshape(height * breadth // 4, 2, 4, width // 2)
    return halves.transpose(0, 2, 1, 3).reshape(height, breadth, width)


def solution(mesh):
    whole = P()
    split = P("lat", "lon", None)
    placed = (split, whole, split) + (whole,) * 10
    return jax.shard_map(local, mesh=mesh, in_specs=placed, out_specs=split, check_vma=False)
```

time: 127 us -> 79.7 us (0.63)
  blocking collectives: 0 us -> 49.7 us
  starting transfers between devices: 40.1 us -> 5.67 us
  local copies, waits for them, and re-layouts: 37.3 us -> 3.67 us
  waiting for transfers between devices: 23.3 us -> 0.01 us
  Pallas kernels: 23.7 us -> 20.4 us
  other arithmetic: 1.41 us -> 0 us
    all_to_all x0 -> x2, blocking collectives: none -> 49.7 us  [exchange(): lax.all_to_all(split, ('lat', 'lon'), split_axis=0, concat_axis=0, tiled=...]
    all_to_all x4 -> x0, starting transfers between devices: 35.8 us -> none  [exchange(): lax.all_to_all(blocks, ('lat', 'lon'), split_axis=0, concat_axis=0, tiled...]
    unnamed x52 -> x0, local copies, waits for them, and re-layouts: 25.5 us -> none
    all_to_all x4 -> x0, waiting for transfers between devices: 16.1 us -> none  [exchange(): lax.all_to_all(blocks, ('lat', 'lon'), split_axis=0, concat_axis=0, tiled...]
    reshape x8 -> x2, local copies, waits for them, and re-layouts: 8.9 us -> 1.58 us  [the longest x1 1.55 us: local(): return halves.transpose(0, 2, 1, 3).reshape(height, breadth, width)]
    ppermute x3 -> x1, waiting for transfers between devices: 7.24 us -> 0.01 us  [from_behind(): return lax.ppermute(block, axis, route)]
    pallas_call x4 -> x3, Pallas kernels: 23.7 us -> 20.4 us  [call(): pl.pallas_call(kernel, out_shape=outs, in_specs=[VMEM_SPEC] * len(in_vmem...]
    ppermute x3 -> x1, starting transfers between devices: 4.23 us -> 5.67 us  [from_behind(): return lax.ppermute(block, axis, route)]
  transfers between devices with their start and end apart: 7 -> 1, of which waited for: 4 -> 0; matrix products, arithmetic and copies ran while one was open for 7% -> 0% of each run, Pallas kernels for 14% -> 10%
where the time goes in v2:
time: 79.7 us; the launch traced here: 79.5 us
  blocking collectives  49.7 us (62%)
  Pallas kernels  20.4 us (26%)
  starting transfers between devices  5.67 us (7%)
  local copies, waits for them, and re-layouts  3.67 us (5%)
    all_to_all x2, blocking collectives, exchange(): lax.all_to_all(split, ('lat', 'lon'), split_axis=0, concat_axis=0, tiled=...  49.7 us
    pallas_call x3, Pallas kernels, call(): pl.pallas_call(kernel, out_shape=outs, in_specs=[VMEM_SPEC] * len(in_vmem...  20.4 us
    ppermute x1, starting transfers between devices, from_behind(): return lax.ppermute(block, axis, route)  5.67 us
  transfers between devices with their start and end apart: 1, of which 0 were waited for; matrix products, arithmetic and copies ran while one was open for 0% of the time, Pallas kernels for 10%

profile of v2, /device:TPU:1, one launch (start us, length us, event | category | flops | bytes accessed | tf_op | source)
XLA Modules:
  0.0 79.5 jit_solution(5184377946393485463)
XLA Ops:
  0.0 1.0 %slice.3 = bf16[16,4,1024]{2,1,0:T(4,128)(2,1)S(1)} slice(bf16[16,32,1024]{2,1,0:T(8,128)(2,1)} %param.13), slice={[0:16], [0:4], [0:1024]} | slice | bytes 262144 | tf_op jit(solution)/shard_map/slice | solution.py:361
  1.0 5.7 %collective-permute-start = (bf16[64,1024]{1,0:T(8,128)(2,1)S(1)}, bf16[64,1024]{1,0:T(8,128)(2,1)S(1)}, u32[]{:S(2)}, u32[]{:S(2)}) collective-permute-start(bf16[64,1024]{1,0:T(8,128)(2,1)S(1)} %reshape.30), channel_id=1, source_target_pairs={{1,0},{2,1},{3,2},{4,3},{5,4},{6,5},{7,6},{0,7},{9,8},{10,9},{11,1... | collective-permute-start | bytes 393224 | tf_op jit(solution)/shard_map/ppermute | solution.py:332
  6.7 8.0 %window_inner.1 = (bf16[384,1024]{1,0:T(8,128)(2,1)S(1)}, bf16[1024,1024]{1,0:T(8,128)(2,1)S(1)}, bf16[1024,1024]{1,0:T(8,128)(2,1)S(1)}, bf16[1024,1024]{1,0:T(8,128)(2,1)S(1)}, bf16[1024,1024]{1,0:T(8,128)(2,1)S(1)}) custom-call(bf16[512,1024]{1,0:T(8,128)(2,1)} %bitcast.14, s32[1,256]{1,0:T(1,128)} %bitcast.18, s32[2,4,4]{2,1,0:T(4,128)} %land_hbm.3, ...), custom_call_target="tpu_custom_call" | custom-call | flops 3221225472 | bytes 10485760 | tf_op jit(solution)/shard_map/window_inner/pallas_call | solution.py:213
  14.7 0.0 collective-permute-done.halo_ref
  14.8 4.8 %window_outer.1 = (bf16[1024,512]{1,0:T(8,128)(2,1)S(1)}, bf16[1024,1024]{1,0:T(8,128)(2,1)S(1)}, bf16[1024,1024]{1,0:T(8,128)(2,1)S(1)}, bf16[1024,1024]{1,0:T(8,128)(2,1)S(1)}, bf16[1024,1024]{1,0:T(8,128)(2,1)S(1)}) custom-call(bf16[384,1024]{1,0:T(8,128)(2,1)S(1)} %get-tuple-element.15.after_ref, bf16[64,1024]{1,0:T(8,128)(2,1)S(1)} %collective-permute-done.halo_ref, ...), custom_call_target="tpu_custom_call" | custom-call | flops 1073741824 | bytes 10485760 | tf_op jit(solution)/shard_map/window_outer/pallas_call | solution.py:213
  19.5 26.4 %all_to_all.10 = bf16[128,8,512]{2,1,0:T(8,128)(2,1)S(1)} all-to-all(bf16[128,8,512]{2,1,0:T(8,128)(2,1)S(1)} %bitcast.10), channel_id=1, replica_groups=mesh['lat'=16,'lon'=8] {'lat','lon'}, dimensions={0} | all-to-all | bytes 2097152 | tf_op jit(solution)/shard_map/all_to_all | solution.py:339
  45.9 7.6 %grid_part.1 = bf16[1024,512]{1,0:T(8,128)(2,1)S(1)} custom-call(bf16[1024,512]{1,0:T(8,128)(2,1)S(1)} %bitcast.11, bf16[1024,1024]{1,0:T(8,128)(2,1)S(1)} %get-tuple-element.21.wq_ref, bf16[1024,1024]{1,0:T(8,128)(2,1)S(1)} %get-tuple-element.22.wk_ref, bf16[1024,1024]{1,0:T(8,128)(2,1)S(1)} %get-tuple-element.23.wv_ref, ...), custom_call_target="tpu_custom_call" | custom-call | flops 4294967296 | bytes 10485760 | tf_op jit(solution)/shard_map/grid_part/pallas_call | solution.py:213
  53.6 23.3 %all_to_all.11 = bf16[128,8,512]{2,1,0:T(8,128)(2,1)S(1)} all-to-all(bf16[128,8,512]{2,1,0:T(8,128)(2,1)S(1)} %bitcast.12), channel_id=1, replica_groups=mesh['lat'=16,'lon'=8] {'lat','lon'}, dimensions={0} | all-to-all | bytes 2097152 | tf_op jit(solution)/shard_map/all_to_all | solution.py:339
  76.8 0.3 reshape_reshape.3
  77.1 0.8 %copy.17 = bf16[128,2,4,512]{3,1,2,0:T(2,128)(2,1)S(1)} copy(bf16[128,2,4,512]{3,2,1,0:T(4,128)(2,1)S(1)} %reshape_reshape.3) | data formatting | bytes 2097152 | tf_op jit(solution)/shard_map/reshape;reshape | solution.py:368
  78.0 1.5 %reshape.35 = bf16[16,32,1024]{2,1,0:T(8,128)(2,1)} reshape(bf16[128,4,2,512]{3,2,1,0:T(2,128)(2,1)S(1)} %bitcast.13) | data formatting | bytes 2097152 | tf_op jit(solution)/shard_map/reshape | solution.py:369
  (1 shorter events, 0.0 us)
Async XLA Ops:
  1.0 13.7 %collective-permute-start = (bf16[64,1024]{1,0:T(8,128)(2,1)S(1)}, bf16[64,1024]{1,0:T(8,128)(2,1)S(1)}, u32[]{:S(2)}, u32[]{:S(2)}) collective-permute-start(bf16[64,1024]{1,0:T(8,128)(2,1)S(1)} %reshape.30), channel_id=1, source_target_pairs={{1,0},{2,1},{3,2},{4,3},{5,4},{6,5},{7,6},{0,7},{9,8},{10,9},{11,1... | collective-permute-start | bytes 393224 | tf_op jit(solution)/shard_map/ppermute | solution.py:332

commit v3 on v2

v3 whole, which is shorter than its diff:
```python
import functools
import math

import jax
import jax.numpy as jnp
from jax import lax
from jax.experimental import pallas as pl
from jax.experimental.pallas import tpu as pltpu
from jax.sharding import PartitionSpec as P

HEADS = 16
GROUPS = 4
WIN = 8
SHIFT = 4
EPSILON = 1e-06
MASKED = -1e30
BF16 = jnp.bfloat16
F32 = jnp.float32
I32 = jnp.int32


def iota(shape, axis):
    return lax.broadcasted_iota(I32, shape, axis)


def one_hot(hits):
    return jnp.where(hits, 1.0, 0.0).astype(BF16)


def matmul(left, right):
    return jnp.dot(left, right, preferred_element_type=F32)


def matmul_nt(left, right):
    return lax.dot_general(left, right, (((1,), (1,)), ((), ())), preferred_element_type=F32)


def norm(rows, gain):
    mean_sq = jnp.mean(rows * rows, axis=-1, keepdims=True)
    return (rows * lax.rsqrt(mean_sq + EPSILON) * gain).astype(BF16)


def usable_bias(pad_ref, wanted_row):
    lanes = wanted_row.shape[1]
    pads = jnp.broadcast_to(pad_ref[...].astype(F32).astype(BF16), (16, pad_ref.shape[1]))
    picks = one_hot(iota((pad_ref.shape[1], lanes), 0) == wanted_row)
    return jnp.where(matmul(pads, picks)[:1] > 0.5, 0.0, MASKED)


def fetch(pairs, sems):
    copies = [
        pltpu.make_async_copy(source, target, sems.at[n]) for n, (source, target) in enumerate(pairs)
    ]
    for copy in copies:
        copy.start()
    return copies


def cross(upper, lower):
    first = iota((1, 8, 1), 1) < 4
    return (
        jnp.where(first, upper, jnp.roll(lower, 4, axis=1)),
        jnp.where(first, jnp.roll(upper, 4, axis=1), lower),
    )


def block_tiles(tiles):
    half = tiles.shape[2] // 2
    return jnp.stack(cross(tiles[:, :, :half], tiles[:, :, half:]), axis=1)


def project(rows, weight, target_ref, factor=None):
    product = matmul(rows, weight[...])
    if factor is not None:
        product = product * factor
    target_ref[...] = product.astype(BF16)


def query_factor(head_size):
    return math.log2(math.e) / math.sqrt(head_size)


def window_attention(bands, gate_of, pad_ref, q_ref, k_ref, v_ref, heads_ref):
    width = q_ref.shape[1]
    head_size = width // HEADS
    quad = 4 * head_size
    first = lax.axis_index("lat") * 16
    key_lane = iota((1, quad), 1) % 64
    biases = [usable_bias(pad_ref, first + band * 8 + key_lane // 8) for band in range(2)]
    head_lane = iota((1, quad), 1) // head_size
    masks = [one_hot(head_lane == h) for h in range(4)]
    ones = one_hot(iota((quad, quad), 0) // 64 == iota((quad, quad), 1) // head_size)
    lower = iota((1, 128), 1) < 64

    def spread(block):
        return jnp.concatenate([block * mask for mask in masks], axis=0)

    for tile, band in enumerate(bands):
        span = slice(tile * 64, (tile + 1) * 64)
        for group in range(GROUPS):
            lanes = slice(group * quad, (group + 1) * quad)
            scores = matmul_nt(q_ref[span, lanes], spread(k_ref[span, lanes])) + biases[band]
            exps = []
            for block in range(2):
                part_scores = scores[:, block * 128 : (block + 1) * 128]
                low = jnp.max(jnp.where(lower, part_scores, -jnp.inf), axis=1, keepdims=True)
                high = jnp.max(jnp.where(lower, -jnp.inf, part_scores), axis=1, keepdims=True)
                exps.append(jnp.exp2(part_scores - jnp.where(lower, low, high)).astype(BF16))
            weight = jnp.concatenate(exps, axis=1)
            total = matmul(weight, ones)
            heads = matmul(weight, spread(v_ref[span, lanes])) / total * gate_of(tile, group)
            heads_ref[span, lanes] = heads.astype(BF16)


def swap_halves(tiles):
    return jnp.roll(tiles, 4, axis=1)


def project_kernel(
    tok_hbm, land_hbm, pad_hbm, gain_hbm, grid_gain_hbm, wq_hbm, wk_hbm, wv_hbm,
    halo_ref, x_ref, edge_ref, gate_ref, pad_ref, gain_ref, grid_gain_ref, wq_ref, wk_ref, wv_ref,
    normed_ref, q_ref,
    tok_ref, land_ref, sems,
):
    copies = fetch(
        [
            (tok_hbm, tok_ref), (land_hbm, land_ref), (gain_hbm, gain_ref),
            (pad_hbm, pad_ref), (grid_gain_hbm, grid_gain_ref),
            (wq_hbm, wq_ref), (wk_hbm, wk_ref), (wv_hbm, wv_ref),
        ],
        sems,
    )
    cells, width = tok_ref.shape
    rows = q_ref.shape[0]
    for copy in copies[:5]:
        copy.wait()
    tiles = tok_ref[...].astype(F32).reshape(16, 4, 8, width)
    first = iota((1, 8, 1), 1) < 4
    pairs = tiles[:, 3].reshape(8, 2, 8, width)
    halo = jnp.where(first, swap_halves(pairs[:, 0]), pairs[:, 1])
    halo_ref[0:64, :] = halo.reshape(64, width).astype(BF16)
    tile_at, group_at = iota((8, width), 0), iota((8, width), 1) // (width // GROUPS)
    gates = jnp.zeros((8, width), F32)
    for tile in range(8):
        for n in range(GROUPS):
            gate = land_ref[tile // 4, tile % 4, n].astype(F32)
            gates = jnp.where((tile_at == tile) & (group_at == n), gate, gates)
    gate_ref[...] = gates
    outer_gates = [gates[3:4], gates[7:8], jnp.zeros((14, width), F32)]
    halo_ref[64:80, :] = jnp.concatenate(outer_gates, axis=0).astype(BF16)
    edge_ref[...] = tiles[:, 0].reshape(128, width).astype(BF16)
    pieces = []
    for band in range(2):
        lines = slice(band * 8, band * 8 + 8)
        for tile_col in range(3):
            pieces.append(
                swap_halves(jnp.where(first, tiles[lines, tile_col + 1], tiles[lines, tile_col]))
            )
    x = jnp.concatenate(pieces, axis=0).reshape(rows, width)
    x_ref[...] = x
    normed = norm(x, gain_ref[...])
    normed_ref[...] = normed
    copies[5].wait()
    project(normed, wq_ref, q_ref, query_factor(width // HEADS))
    for copy in copies[6:]:
        copy.wait()


def inner_kernel(
    x_ref, normed_ref, q_ref, wk_ref, wv_ref, pad_ref, gate_ref,
    wo_hbm, gq_hbm, gk_hbm, gv_hbm, go_hbm,
    out_ref, wo_ref, gq_ref, gk_ref, gv_ref, go_ref,
    k_ref, v_ref, heads_ref, sems,
):
    copies = fetch(
        [
            (wo_hbm, wo_ref), (gq_hbm, gq_ref), (gk_hbm, gk_ref), (gv_hbm, gv_ref),
            (go_hbm, go_ref),
        ],
        sems,
    )
    rows, width = heads_ref.shape
    quad = width // GROUPS
    normed = normed_ref[...]
    project(normed, wk_ref, k_ref)
    project(normed, wv_ref, v_ref)

    def gate_of(tile, group):
        row = tile // 3 * 4 + tile % 3
        return gate_ref[row : row + 1, group * quad : (group + 1) * quad]

    window_attention([0, 0, 0, 1, 1, 1], gate_of, pad_ref, q_ref, k_ref, v_ref, heads_ref)
    copies[0].wait()
    after = x_ref[...] + matmul(heads_ref[...], wo_ref[...])
    blocks = block_tiles(after.reshape(rows // 8, 8, width))
    out_ref[...] = blocks.reshape(2 * rows, width // 2).astype(BF16)
    for copy in copies[1:]:
        copy.wait()


def outer_kernel(
    inner_ref, halo_ref, edge_ref, gain_ref, wq_ref, wk_ref, wv_ref, wo_ref, pad_ref,
    out_ref, q_ref, k_ref, v_ref, heads_ref,
):
    rows, width = heads_ref.shape
    first = iota((1, 8, 1), 1) < 4
    own = edge_ref[...].astype(F32).reshape(8, 2, 8, width)
    halo = halo_ref[0:64, :].astype(F32).reshape(8, 8, width)
    even = jnp.where(first, halo, swap_halves(own[:, 0]))
    odd = swap_halves(jnp.where(first, own[:, 1], halo))
    gates = halo_ref[64:80, :].astype(F32)
    x = jnp.stack([even, odd], axis=1).reshape(rows, width)
    normed = norm(x, gain_ref[...])
    project(normed, wq_ref, q_ref, query_factor(width // HEADS))
    project(normed, wk_ref, k_ref)
    project(normed, wv_ref, v_ref)

    def gate_of(tile, group):
        return gates[tile : tile + 1, group * (width // GROUPS) : (group + 1) * (width // GROUPS)]

    window_attention([0, 1], gate_of, pad_ref, q_ref, k_ref, v_ref, heads_ref)
    after = x + matmul(heads_ref[...], wo_ref[...])
    outer = block_tiles(after.reshape(16, 8, width))
    inner = inner_ref[...].astype(F32).reshape(2, 3, 8, 2, 8, width // 2)
    for band in range(2):
        lines = slice(band * 8, band * 8 + 8)
        ordered = [outer[lines, 1]]
        for tile_col in range(3):
            ordered += [inner[band, tile_col, :, 0], inner[band, tile_col, :, 1]]
        ordered.append(outer[lines, 0])
        blocks = jnp.stack(ordered, axis=1).reshape(512, width // 2)
        out_ref[band * 512 : (band + 1) * 512, :] = blocks.astype(BF16)


def in_hbm(arrays):
    return [pltpu.with_memory_space_constraint(a, pltpu.HBM) for a in arrays]


VMEM_SPEC = pl.BlockSpec(memory_space=pltpu.VMEM)
HBM_SPEC = pl.BlockSpec(memory_space=pltpu.HBM)


def call(kernel, name, outs, in_vmem, from_hbm, scratch, rows, exps):
    width = 1024
    return pl.pallas_call(
        kernel,
        out_shape=outs,
        in_specs=[VMEM_SPEC] * len(in_vmem) + [HBM_SPEC] * len(from_hbm),
        out_specs=[VMEM_SPEC] * len(outs),
        scratch_shapes=scratch,
        compiler_params=pltpu.CompilerParams(vmem_limit_bytes=28 * 2**20),
        cost_estimate=pl.CostEstimate(
            flops=8 * rows * width * width, bytes_accessed=10 * 2**20, transcendentals=exps
        ),
        name=name,
    )(*in_vmem, *in_hbm(from_hbm))


def window_part(tokens, pads, land_sea, gain, grid_gain, weights, grid_weights):
    cells, width = tokens.shape
    inner, outer = cells * 3 // 4, cells // 4
    weight = pltpu.VMEM((width, width), BF16)
    rows = pltpu.VMEM((inner, width), BF16)
    halo, x, edge, gates, pads_held, win_gain, gain_held, wq, wk, wv, normed, q = call(
        project_kernel,
        "window_project",
        [
            jax.ShapeDtypeStruct((cells // 8 + 16, width), BF16),
            pltpu.VMEM((inner, width), F32),
            pltpu.VMEM((outer, width), BF16),
            pltpu.VMEM((8, width), F32),
            pltpu.VMEM(pads.shape, I32),
            pltpu.VMEM(gain.shape, F32),
            pltpu.VMEM(grid_gain.shape, F32),
        ]
        + [weight] * 3
        + [rows] * 2,
        [],
        [tokens, land_sea, pads, gain, grid_gain, *weights[:3]],
        [
            pltpu.VMEM((cells, width), BF16),
            pltpu.SMEM(land_sea.shape, I32),
            pltpu.SemaphoreType.DMA((8,)),
        ],
        inner,
        0,
    )
    halo = from_behind(halo, "lon", 1)
    inside, wo, *grid_held = call(
        inner_kernel,
        "window_inner",
        [pltpu.VMEM((2 * inner, width // 2), BF16)] + [weight] * 5,
        [x, normed, q, wk, wv, pads_held, gates],
        [weights[3], *grid_weights],
        [rows] * 3 + [pltpu.SemaphoreType.DMA((5,))],
        inner,
        inner * 1024,
    )
    blocks = call(
        outer_kernel,
        "window_outer",
        [jax.ShapeDtypeStruct((2 * cells, width // 2), BF16)],
        [inside, halo, edge, win_gain, wq, wk, wv, wo, pads_held],
        [],
        [pltpu.VMEM((outer, width), BF16)] * 4,
        outer,
        outer * 1024,
    )[0]
    grid_held = [pads_held, gain_held, *grid_held]
    return blocks, grid_held


def grid_kernel(
    block_ref, pad_ref, gain_ref, wq_ref, wk_ref, wv_ref, wo_ref,
    out_ref, wide_ref, x_ref, normed_ref, q_ref, k_ref, v_ref, heads_ref,
):
    rows, width = q_ref.shape
    members = 128
    groups = rows // members
    head_size = width // HEADS
    pair = 2 * head_size
    chunks = wide_ref.shape[0]
    for chunk in range(chunks):
        wide_ref[chunk] = block_ref[:, chunk * 128 : (chunk + 1) * 128].astype(F32)
    lanes_of = [
        (slice(n * 128, (n + 1) * 128), n % chunks, n // chunks * groups)
        for n in range(2 * chunks)
    ]
    for group in range(groups):
        span = slice(group * members, (group + 1) * members)
        for lanes, chunk, start in lanes_of:
            x_ref[span, lanes] = wide_ref[chunk, pl.ds(start + group, members, stride=8), :]
        normed_ref[span, :] = norm(x_ref[span, :], gain_ref[...])
    normed = normed_ref[...]
    project(normed, wq_ref, q_ref, query_factor(head_size))
    project(normed, wk_ref, k_ref)
    project(normed, wv_ref, v_ref)
    key_lane = iota((1, 2 * members), 1) % members
    bias = usable_bias(pad_ref, (key_lane // 8) * 16 + lax.axis_index("lat"))
    masks = [one_hot(iota((1, pair), 1) // head_size == h) for h in range(2)]
    ones = one_hot(
        iota((2 * members, pair), 0) // members == iota((2 * members, pair), 1) // head_size
    )

    def spread(block):
        return jnp.concatenate([block * mask for mask in masks], axis=0)

    for group in range(groups):
        span = slice(group * members, (group + 1) * members)
        for two in range(HEADS // 2):
            lanes = slice(two * pair, (two + 1) * pair)
            scores = matmul_nt(q_ref[span, lanes], spread(k_ref[span, lanes])) + bias
            exps = []
            for half in range(2):
                head_scores = scores[:, half * members : (half + 1) * members]
                largest = jnp.max(head_scores, axis=1, keepdims=True)
                exps.append(jnp.exp2(head_scores - largest).astype(BF16))
            weight = jnp.concatenate(exps, axis=1)
            both = jnp.concatenate([spread(v_ref[span, lanes]), ones], axis=1)
            sums = matmul(weight, both)
            heads_ref[span, lanes] = (sums[:, :pair] / sums[:, pair:]).astype(BF16)
    wrapped = lax.axis_index("lon") == lax.axis_size("lon") - 1
    mixed = x_ref[...] + matmul(heads_ref[...], wo_ref[...])
    for group in range(groups):
        span = slice(group * members, (group + 1) * members)
        tiles = mixed[span].reshape(members // 8, 8, width)
        home = jnp.where(wrapped, jnp.roll(tiles, -1, axis=1), tiles).reshape(members, width)
        for lanes, chunk, start in lanes_of:
            wide_ref[chunk, pl.ds(start + group, members, stride=8), :] = home[:, lanes]
    for chunk in range(chunks):
        out_ref[:, chunk * 128 : (chunk + 1) * 128] = wide_ref[chunk].astype(BF16)


def grid_part(blocks, held):
    rows, width = blocks.shape[0] // 2, blocks.shape[1] * 2
    return call(
        grid_kernel,
        "grid_part",
        [jax.ShapeDtypeStruct(blocks.shape, BF16)],
        [blocks, *held],
        [],
        [
            pltpu.VMEM((blocks.shape[1] // 128, blocks.shape[0], 128), F32),
            pltpu.VMEM((rows, width), F32),
        ]
        + [pltpu.VMEM((rows, width), BF16)] * 5,
        rows,
        rows * 2048,
    )[0]


def final_kernel(block_ref, out_hbm, out_ref, sems):
    rows, width = out_ref.shape
    steps = 4
    part = rows // steps
    copies = []
    for step in range(steps):
        span = slice(step * part, (step + 1) * part)
        blocks = block_ref[2 * step * part : 2 * (step + 1) * part, :].astype(F32)
        tiles = blocks.reshape(part // 8, 2, 8, width // 2)
        whole = jnp.concatenate(cross(tiles[:, 0], tiles[:, 1]), axis=2)
        out_ref[span, :] = whole.reshape(part, width).astype(BF16)
        copy = pltpu.make_async_copy(out_ref.at[span], out_hbm.at[span], sems.at[step])
        copy.start()
        copies.append(copy)
    for copy in copies:
        copy.wait()


def final_part(blocks):
    rows, width = blocks.shape[0] // 2, blocks.shape[1] * 2
    return pl.pallas_call(
        final_kernel,
        out_shape=jax.ShapeDtypeStruct((rows, width), BF16),
        in_specs=[VMEM_SPEC],
        out_specs=HBM_SPEC,
        scratch_shapes=[pltpu.VMEM((rows, width), BF16), pltpu.SemaphoreType.DMA((4,))],
        compiler_params=pltpu.CompilerParams(vmem_limit_bytes=16 * 2**20),
        name="final_part",
    )(blocks)


def from_behind(block, axis, distance):
    devices = range(lax.axis_size(axis))
    route = [((i - distance) % len(devices), i) for i in devices]
    return lax.ppermute(block, axis, route)


def exchange(blocks):
    count, width = blocks.shape
    members = lax.axis_size("lat") * lax.axis_size("lon")
    split = blocks.reshape(members, count // members, width)
    moved = lax.all_to_all(split, ("lat", "lon"), split_axis=0, concat_axis=0, tiled=True)
    return moved.reshape(count, width)


def local(
    tokens,
    pad_rows,
    land_sea,
    win_gain,
    win_query,
    win_key,
    win_value,
    win_out,
    grid_gain,
    grid_query,
    grid_key,
    grid_value,
    grid_out,
):
    height, breadth, width = tokens.shape
    flat = tokens.reshape(height * breadth, width)
    pads = pad_rows.reshape(1, -1)
    win_weights = (win_query, win_key, win_value, win_out)
    grid_weights = (grid_query, grid_key, grid_value, grid_out)
    win_gain, grid_gain = win_gain.reshape(1, -1), grid_gain.reshape(1, -1)
    blocks, held = window_part(
        flat, pads, land_sea, win_gain, grid_gain, win_weights, grid_weights
    )
    mixed = exchange(grid_part(exchange(blocks), held))
    return final_part(mixed).reshape(height, breadth, width)


def solution(mesh):
    whole = P()
    split = P("lat", "lon", None)
    placed = (split, whole, split) + (whole,) * 10
    return jax.shard_map(local, mesh=mesh, in_specs=placed, out_specs=split, check_vma=False)
```

time: 79.7 us -> 75.2 us (0.944)
  local copies, waits for them, and re-layouts: 3.67 us -> 0 us
  starting transfers between devices: 5.67 us -> 2.54 us
  blocking collectives: 49.7 us -> 51.7 us
  waiting for transfers between devices: 0.01 us -> 1.29 us
  Pallas kernels: 20.4 us -> 19.3 us
    ppermute x1, starting transfers between devices: 5.67 us -> 2.54 us  [from_behind(): return lax.ppermute(block, axis, route)]
    pallas_call x3 -> x4, Pallas kernels: 20.4 us -> 18.2 us  [call(): pl.pallas_call(kernel, out_shape=outs, in_specs=[VMEM_SPEC] * len(in_vmem...]
    all_to_all x2, blocking collectives: 49.7 us -> 51.7 us  [exchange(): lax.all_to_all(split, ('lat', 'lon'), split_axis=0, concat_axis=0, tiled=...]
    reshape x2 -> x0, local copies, waits for them, and re-layouts: 1.58 us -> none  [the longest x1 1.55 us: local(): return halves.transpose(0, 2, 1, 3).reshape(height, breadth, width)]
    ppermute x1, waiting for transfers between devices: 0.01 us -> 1.29 us  [from_behind(): return lax.ppermute(block, axis, route)]
    another operation x2 -> x0, local copies, waits for them, and re-layouts: 1.1 us -> none  [local(): halves = mixed.reshape(height * breadth // 4, 2, 4, width // 2)]
    pallas_call x0 -> x1, Pallas kernels: none -> 1.06 us  [final_part(): pl.pallas_call(final_kernel, out_shape=jax.ShapeDtypeStruct((rows, width)...]
    slice x1 -> x0, local copies, waits for them, and re-layouts: 0.99 us -> none  [local(): tokens[:, :SHIFT].reshape(height * SHIFT, width)]
  transfers between devices with their start and end apart: 1 -> 1, of which waited for: 0 -> 1; matrix products, arithmetic and copies ran while one was open for 0% -> 0% of each run, Pallas kernels for 10% -> 8%
where the time goes in v3:
time: 75.2 us; the launch traced here: 75 us
  blocking collectives  51.7 us (69%)
  Pallas kernels  19.3 us (26%)
  starting transfers between devices  2.54 us (3%)
  waiting for transfers between devices  1.29 us (2%)
    all_to_all x2, blocking collectives, exchange(): lax.all_to_all(split, ('lat', 'lon'), split_axis=0, concat_axis=0, tiled=...  51.7 us
    pallas_call x4, Pallas kernels, call(): pl.pallas_call(kernel, out_shape=outs, in_specs=[VMEM_SPEC] * len(in_vmem...  18.2 us
    ppermute x1, starting transfers between devices, from_behind(): return lax.ppermute(block, axis, route)  2.54 us
  transfers between devices with their start and end apart: 1, of which 1 were waited for; matrix products, arithmetic and copies ran while one was open for 0% of the time, Pallas kernels for 8%

profile of v3, /device:TPU:1, one launch (start us, length us, event | category | flops | bytes accessed | tf_op | source)
XLA Modules:
  0.0 75.0 jit_solution(15939289011835334)
XLA Ops:
  0.0 3.3 %window_project.1 = (bf16[80,1024]{1,0:T(8,128)(2,1)S(1)}, f32[384,1024]{1,0:T(8,128)S(1)}, bf16[128,1024]{1,0:T(8,128)(2,1)S(1)}, f32[8,1024]{1,0:T(8,128)S(1)}...) custom-call(bf16[512,1024]{1,0:T(8,128)(2,1)} %bitcast.13, ...), custom_call_target="tpu_custom_call" | custom-call | flops 3221225472 | bytes 10485760 | tf_op jit(solution)/shard_map/window_project/pallas_call | solution.py:245
  3.3 2.5 %collective-permute-start = (bf16[80,1024]{1,0:T(8,128)(2,1)S(1)}, bf16[80,1024]{1,0:T(8,128)(2,1)S(1)}, u32[]{:S(2)}, u32[]{:S(2)}) collective-permute-start(bf16[80,1024]{1,0:T(8,128)(2,1)S(1)} %get-tuple-element.31), channel_id=1, source_target_pairs={{7,0},{0,1},{1,2},{2,3},{3,4},{4,5},{5,6},{6,7},{15,8},{8,9},{9,10... | collective-permute-start | bytes 491528 | tf_op jit(solution)/shard_map/ppermute | solution.py:426
  5.8 5.8 %window_inner.1 = (bf16[768,512]{1,0:T(8,128)(2,1)S(1)}, bf16[1024,1024]{1,0:T(8,128)(2,1)S(1)}, bf16[1024,1024]{1,0:T(8,128)(2,1)S(1)}, bf16[1024,1024]{1,0:T(8...) custom-call(f32[384,1024]{1,0:T(8,128)S(1)} %get-tuple-element.23.x_ref, ...), custom_call_target="tpu_custom_call" | custom-call | flops 3221225472 | bytes 10485760 | tf_op jit(solution)/shard_map/window_inner/pallas_call | solution.py:245
  11.6 1.3 %collective-permute-done.halo_ref = bf16[80,1024]{1,0:T(8,128)(2,1)S(1)} collective-permute-done((bf16[80,1024]{1,0:T(8,128)(2,1)S(1)}, bf16[80,1024]{1,0:T(8,128)(2,1)S(1)}, u32[]{:S(2)}, u32[]{:S(2)}) %collective-permute-start) | collective-permute-done | bytes 163872 | tf_op jit(solution)/shard_map/ppermute | solution.py:426
  12.9 2.4 %window_outer.1 = bf16[1024,512]{1,0:T(8,128)(2,1)S(1)} custom-call(bf16[768,512]{1,0:T(8,128)(2,1)S(1)} %get-tuple-element.30.inner_ref, bf16[80,1024]{1,0:T(8,128)(2,1)S(1)} %collective-permute-done.halo_ref, bf16[128,1024]{1,0:T(8,128)(2,1)S(1)} %get-tuple-element.32.edge_ref, f32[1,1024]{1,0:T(1,128)S(1)} %get-tuple-element.33.gain_ref, ...), custom_call_target="tpu_custom_call" | custom-call | flops 1073741824 | bytes 10485760 | tf_op jit(solution)/shard_map/window_outer/pallas_call | solution.py:245
  15.3 28.5 %all_to_all.10 = bf16[128,8,512]{2,1,0:T(8,128)(2,1)S(1)} all-to-all(bf16[128,8,512]{2,1,0:T(8,128)(2,1)S(1)} %bitcast.9), channel_id=1, replica_groups=mesh['lat'=16,'lon'=8] {'lat','lon'}, dimensions={0} | all-to-all | bytes 2097152 | tf_op jit(solution)/shard_map/all_to_all | solution.py:433
  43.8 6.8 %grid_part.1 = bf16[1024,512]{1,0:T(8,128)(2,1)S(1)} custom-call(bf16[1024,512]{1,0:T(8,128)(2,1)S(1)} %bitcast.11, s32[1,256]{1,0:T(1,128)S(1)} %get-tuple-element.28.pad_ref, f32[1,1024]{1,0:T(1,128)S(1)} %get-tuple-element.36.gain_ref, bf16[1024,1024]{1,0:T(8,128)(2,1)S(1)} %get-tuple-element.37.wq_ref, bf16[1024,1024]{1,0:T(8,128)(2,1)S(1)} %get-tuple-element.38.wk_ref, ...), custom_call_target="tpu_custom_call" | custom-call | flops 4294967296 | bytes 10485760 | tf_op jit(solution)/shard_map/grid_part/pallas_call | solution.py:245
  50.5 23.3 %all_to_all.11 = bf16[128,8,512]{2,1,0:T(8,128)(2,1)S(1)} all-to-all(bf16[128,8,512]{2,1,0:T(8,128)(2,1)S(1)} %bitcast.12), channel_id=1, replica_groups=mesh['lat'=16,'lon'=8] {'lat','lon'}, dimensions={0} | all-to-all | bytes 2097152 | tf_op jit(solution)/shard_map/all_to_all | solution.py:433
  73.8 1.1 %final_part.1 = bf16[512,1024]{1,0:T(8,128)(2,1)} custom-call(bf16[1024,512]{1,0:T(8,128)(2,1)S(1)} %bitcast.10), custom_call_target="tpu_custom_call" | custom-call | tf_op jit(solution)/shard_map/final_part/pallas_call | solution.py:412
Async XLA Ops:
  3.3 9.6 %collective-permute-start = (bf16[80,1024]{1,0:T(8,128)(2,1)S(1)}, bf16[80,1024]{1,0:T(8,128)(2,1)S(1)}, u32[]{:S(2)}, u32[]{:S(2)}) collective-permute-start(bf16[80,1024]{1,0:T(8,128)(2,1)S(1)} %get-tuple-element.31), channel_id=1, source_target_pairs={{7,0},{0,1},{1,2},{2,3},{3,4},{4,5},{5,6},{6,7},{15,8},{8,9},{9,10... | collective-permute-start | bytes 491528 | tf_op jit(solution)/shard_map/ppermute | solution.py:426

commit v4 on v3

--- a/solution.py
+++ b/solution.py
@@ -95,20 +95,29 @@
     def spread(block):
         return jnp.concatenate([block * mask for mask in masks], axis=0)
 
-    for tile, band in enumerate(bands):
+    def weight_of(tile, group):
         span = slice(tile * 64, (tile + 1) * 64)
-        for group in range(GROUPS):
+        lanes = slice(group * quad, (group + 1) * quad)
+        scores = matmul_nt(q_ref[span, lanes], spread(k_ref[span, lanes])) + biases[bands[tile]]
+        exps = []
+        for block in range(2):
+            part_scores = scores[:, block * 128 : (block + 1) * 128]
+            low = jnp.max(jnp.where(lower, part_scores, -jnp.inf), axis=1, keepdims=True)
+            high = jnp.max(jnp.where(lower, -jnp.inf, part_scores), axis=1, keepdims=True)
+            exps.append(jnp.exp2(part_scores - jnp.where(lower, low, high)).astype(BF16))
+        return jnp.concatenate(exps, axis=1)
+
+    units = [(tile, group) for group in range(GROUPS) for tile in range(len(bands))]
+    size = min(8, len(units))
+    for start in range(0, len(units), size):
+        batch = units[start : start + size]
+        weights = [weight_of(*unit) for unit in batch]
+        totals = matmul(jnp.concatenate(weights, axis=0), ones)
+        for at, (tile, group) in enumerate(batch):
+            span = slice(tile * 64, (tile + 1) * 64)
             lanes = slice(group * quad, (group + 1) * quad)
-            scores = matmul_nt(q_ref[span, lanes], spread(k_ref[span, lanes])) + biases[band]
-            exps = []
-            for block in range(2):
-                part_scores = scores[:, block * 128 : (block + 1) * 128]
-                low = jnp.max(jnp.where(lower, part_scores, -jnp.inf), axis=1, keepdims=True)
-                high = jnp.max(jnp.where(lower, -jnp.inf, part_scores), axis=1, keepdims=True)
-                exps.append(jnp.exp2(part_scores - jnp.where(lower, low, high)).astype(BF16))
-            weight = jnp.concatenate(exps, axis=1)
-            total = matmul(weight, ones)
-            heads = matmul(weight, spread(v_ref[span, lanes])) / total * gate_of(tile, group)
+            total = totals[at * 64 : (at + 1) * 64]
+            heads = matmul(weights[at], spread(v_ref[span, lanes])) / total * gate_of(tile, group)
             heads_ref[span, lanes] = heads.astype(BF16)
 
 

time: 75.2 us -> 74.1 us (0.985)
  Pallas kernels: 19.3 us -> 18.2 us
  waiting for transfers between devices: 1.29 us -> 2.17 us
  blocking collectives: 51.7 us -> 50.9 us
    pallas_call x4, Pallas kernels: 18.2 us -> 17.2 us  [call(): pl.pallas_call(kernel, out_shape=outs, in_specs=[VMEM_SPEC] * len(in_vmem...]
    ppermute x1, waiting for transfers between devices: 1.29 us -> 2.17 us  [from_behind(): return lax.ppermute(block, axis, route)]
    all_to_all x2, blocking collectives: 51.7 us -> 50.9 us  [exchange(): lax.all_to_all(split, ('lat', 'lon'), split_axis=0, concat_axis=0, tiled=...]
  transfers between devices with their start and end apart: 1 -> 1, of which waited for: 1 -> 1; matrix products, arithmetic and copies ran while one was open for 0% -> 0% of each run, Pallas kernels for 8% -> 7%
where the time goes in v4:
time: 74.1 us; the launch traced here: 74 us
  blocking collectives  50.9 us (69%)
  Pallas kernels  18.2 us (25%)
  starting transfers between devices  2.54 us (3%)
  waiting for transfers between devices  2.17 us (3%)
    all_to_all x2, blocking collectives, exchange(): lax.all_to_all(split, ('lat', 'lon'), split_axis=0, concat_axis=0, tiled=...  50.9 us
    pallas_call x4, Pallas kernels, call(): pl.pallas_call(kernel, out_shape=outs, in_specs=[VMEM_SPEC] * len(in_vmem...  17.2 us
    ppermute x1, starting transfers between devices, from_behind(): return lax.ppermute(block, axis, route)  2.54 us
    ppermute x1, waiting for transfers between devices, from_behind(): return lax.ppermute(block, axis, route)  2.17 us
  transfers between devices with their start and end apart: 1, of which 1 were waited for; matrix products, arithmetic and copies ran while one was open for 0% of the time, Pallas kernels for 7%

profile of v4, /device:TPU:1, one launch (start us, length us, event | category | flops | bytes accessed | tf_op | source)
XLA Modules:
  0.0 74.0 jit_solution(1182716709349805806)
XLA Ops:
  0.0 3.3 %window_project.1 = (bf16[80,1024]{1,0:T(8,128)(2,1)S(1)}, f32[384,1024]{1,0:T(8,128)S(1)}, bf16[128,1024]{1,0:T(8,128)(2,1)S(1)}, f32[8,1024]{1,0:T(8,128)S(1)}...) custom-call(bf16[512,1024]{1,0:T(8,128)(2,1)} %bitcast.13, ...), custom_call_target="tpu_custom_call" | custom-call | flops 3221225472 | bytes 10485760 | tf_op jit(solution)/shard_map/window_project/pallas_call | solution.py:254
  3.3 2.5 %collective-permute-start = (bf16[80,1024]{1,0:T(8,128)(2,1)S(1)}, bf16[80,1024]{1,0:T(8,128)(2,1)S(1)}, u32[]{:S(2)}, u32[]{:S(2)}) collective-permute-start(bf16[80,1024]{1,0:T(8,128)(2,1)S(1)} %get-tuple-element.31), channel_id=1, source_target_pairs={{7,0},{0,1},{1,2},{2,3},{3,4},{4,5},{5,6},{6,7},{15,8},{8,9},{9,10... | collective-permute-start | bytes 491528 | tf_op jit(solution)/shard_map/ppermute | solution.py:435
  5.8 4.9 %window_inner.1 = (bf16[768,512]{1,0:T(8,128)(2,1)S(1)}, bf16[1024,1024]{1,0:T(8,128)(2,1)S(1)}, bf16[1024,1024]{1,0:T(8,128)(2,1)S(1)}, bf16[1024,1024]{1,0:T(8...) custom-call(f32[384,1024]{1,0:T(8,128)S(1)} %get-tuple-element.23.x_ref, ...), custom_call_target="tpu_custom_call" | custom-call | flops 3221225472 | bytes 10485760 | tf_op jit(solution)/shard_map/window_inner/pallas_call | solution.py:254
  10.7 2.2 %collective-permute-done.halo_ref = bf16[80,1024]{1,0:T(8,128)(2,1)S(1)} collective-permute-done((bf16[80,1024]{1,0:T(8,128)(2,1)S(1)}, bf16[80,1024]{1,0:T(8,128)(2,1)S(1)}, u32[]{:S(2)}, u32[]{:S(2)}) %collective-permute-start) | collective-permute-done | bytes 163872 | tf_op jit(solution)/shard_map/ppermute | solution.py:435
  12.9 2.2 %window_outer.1 = bf16[1024,512]{1,0:T(8,128)(2,1)S(1)} custom-call(bf16[768,512]{1,0:T(8,128)(2,1)S(1)} %get-tuple-element.30.inner_ref, bf16[80,1024]{1,0:T(8,128)(2,1)S(1)} %collective-permute-done.halo_ref, bf16[128,1024]{1,0:T(8,128)(2,1)S(1)} %get-tuple-element.32.edge_ref, f32[1,1024]{1,0:T(1,128)S(1)} %get-tuple-element.33.gain_ref, ...), custom_call_target="tpu_custom_call" | custom-call | flops 1073741824 | bytes 10485760 | tf_op jit(solution)/shard_map/window_outer/pallas_call | solution.py:254
  15.1 27.6 %all_to_all.10 = bf16[128,8,512]{2,1,0:T(8,128)(2,1)S(1)} all-to-all(bf16[128,8,512]{2,1,0:T(8,128)(2,1)S(1)} %bitcast.9), channel_id=1, replica_groups=mesh['lat'=16,'lon'=8] {'lat','lon'}, dimensions={0} | all-to-all | bytes 2097152 | tf_op jit(solution)/shard_map/all_to_all | solution.py:442
  42.7 6.8 %grid_part.1 = bf16[1024,512]{1,0:T(8,128)(2,1)S(1)} custom-call(bf16[1024,512]{1,0:T(8,128)(2,1)S(1)} %bitcast.11, s32[1,256]{1,0:T(1,128)S(1)} %get-tuple-element.28.pad_ref, f32[1,1024]{1,0:T(1,128)S(1)} %get-tuple-element.36.gain_ref, bf16[1024,1024]{1,0:T(8,128)(2,1)S(1)} %get-tuple-element.37.wq_ref, bf16[1024,1024]{1,0:T(8,128)(2,1)S(1)} %get-tuple-element.38.wk_ref, ...), custom_call_target="tpu_custom_call" | custom-call | flops 4294967296 | bytes 10485760 | tf_op jit(solution)/shard_map/grid_part/pallas_call | solution.py:254
  49.5 23.3 %all_to_all.11 = bf16[128,8,512]{2,1,0:T(8,128)(2,1)S(1)} all-to-all(bf16[128,8,512]{2,1,0:T(8,128)(2,1)S(1)} %bitcast.12), channel_id=1, replica_groups=mesh['lat'=16,'lon'=8] {'lat','lon'}, dimensions={0} | all-to-all | bytes 2097152 | tf_op jit(solution)/shard_map/all_to_all | solution.py:442
  72.8 1.1 %final_part.1 = bf16[512,1024]{1,0:T(8,128)(2,1)} custom-call(bf16[1024,512]{1,0:T(8,128)(2,1)S(1)} %bitcast.10), custom_call_target="tpu_custom_call" | custom-call | tf_op jit(solution)/shard_map/final_part/pallas_call | solution.py:421
Async XLA Ops:
  3.3 9.6 %collective-permute-start = (bf16[80,1024]{1,0:T(8,128)(2,1)S(1)}, bf16[80,1024]{1,0:T(8,128)(2,1)S(1)}, u32[]{:S(2)}, u32[]{:S(2)}) collective-permute-start(bf16[80,1024]{1,0:T(8,128)(2,1)S(1)} %get-tuple-element.31), channel_id=1, source_target_pairs={{7,0},{0,1},{1,2},{2,3},{3,4},{4,5},{5,6},{6,7},{15,8},{8,9},{9,10... | collective-permute-start | bytes 491528 | tf_op jit(solution)/shard_map/ppermute | solution.py:435

commit v5 on v4

--- a/solution.py
+++ b/solution.py
@@ -108,10 +108,9 @@
         return jnp.concatenate(exps, axis=1)
 
     units = [(tile, group) for group in range(GROUPS) for tile in range(len(bands))]
-    size = min(8, len(units))
-    for start in range(0, len(units), size):
-        batch = units[start : start + size]
-        weights = [weight_of(*unit) for unit in batch]
+    batches = [units[at : at + 4] for at in range(0, len(units), 4)]
+
+    def finish(batch, weights):
         totals = matmul(jnp.concatenate(weights, axis=0), ones)
         for at, (tile, group) in enumerate(batch):
             span = slice(tile * 64, (tile + 1) * 64)
@@ -119,6 +118,14 @@
             total = totals[at * 64 : (at + 1) * 64]
             heads = matmul(weights[at], spread(v_ref[span, lanes])) / total * gate_of(tile, group)
             heads_ref[span, lanes] = heads.astype(BF16)
+
+    last = None
+    for batch in batches:
+        weights = [weight_of(*unit) for unit in batch]
+        if last is not None:
+            finish(*last)
+        last = (batch, weights)
+    finish(*last)
 
 
 def swap_halves(tiles):
@@ -330,7 +337,7 @@
     pair = 2 * head_size
     chunks = wide_ref.shape[0]
     for chunk in range(chunks):
-        wide_ref[chunk] = block_ref[:, chunk * 128 : (chunk + 1) * 128].astype(F32)
+        wide_ref[chunk, : 2 * rows] = block_ref[:, chunk * 128 : (chunk + 1) * 128].astype(F32)
     lanes_of = [
         (slice(n * 128, (n + 1) * 128), n % chunks, n // chunks * groups)
         for n in range(2 * chunks)
@@ -377,7 +384,7 @@
         for lanes, chunk, start in lanes_of:
             wide_ref[chunk, pl.ds(start + group, members, stride=8), :] = home[:, lanes]
     for chunk in range(chunks):
-        out_ref[:, chunk * 128 : (chunk + 1) * 128] = wide_ref[chunk].astype(BF16)
+        out_ref[:, chunk * 128 : (chunk + 1) * 128] = wide_ref[chunk, : 2 * rows].astype(BF16)
 
 
 def grid_part(blocks, held):
@@ -389,7 +396,7 @@
         [blocks, *held],
         [],
         [
-            pltpu.VMEM((blocks.shape[1] // 128, blocks.shape[0], 128), F32),
+            pltpu.VMEM((blocks.shape[1] // 128, blocks.shape[0] + 8, 128), F32),
             pltpu.VMEM((rows, width), F32),
         ]
         + [pltpu.VMEM((rows, width), BF16)] * 5,

time: 74.1 us -> 74.8 us (level)
  Pallas kernels: 18.2 us -> 19 us
  waiting for transfers between devices: 2.17 us -> 1.41 us
    ppermute x1, waiting for transfers between devices: 2.17 us -> 1.41 us  [from_behind(): return lax.ppermute(block, axis, route)]
  transfers between devices with their start and end apart: 1 -> 1, of which waited for: 1 -> 1; matrix products, arithmetic and copies ran while one was open for 0% -> 0% of each run, Pallas kernels for 7% -> 8%
where the time goes in v5:
time: 74.8 us; the launch traced here: 74.7 us
  blocking collectives  51.6 us (69%)
  Pallas kernels  19 us (25%)
  starting transfers between devices  2.54 us (3%)
  waiting for transfers between devices  1.41 us (2%)
    all_to_all x2, blocking collectives, exchange(): lax.all_to_all(split, ('lat', 'lon'), split_axis=0, concat_axis=0, tiled=...  51.6 us
    pallas_call x4, Pallas kernels, call(): pl.pallas_call(kernel, out_shape=outs, in_specs=[VMEM_SPEC] * len(in_vmem...  17.9 us
    ppermute x1, starting transfers between devices, from_behind(): return lax.ppermute(block, axis, route)  2.54 us
  transfers between devices with their start and end apart: 1, of which 1 were waited for; matrix products, arithmetic and copies ran while one was open for 0% of the time, Pallas kernels for 8%

profile of v5, /device:TPU:1, one launch (start us, length us, event | category | flops | bytes accessed | tf_op | source)
XLA Modules:
  0.0 74.7 jit_solution(5813334932735026897)
XLA Ops:
  0.0 3.3 %window_project.1 = (bf16[80,1024]{1,0:T(8,128)(2,1)S(1)}, f32[384,1024]{1,0:T(8,128)S(1)}, bf16[128,1024]{1,0:T(8,128)(2,1)S(1)}, f32[8,1024]{1,0:T(8,128)S(1)}...) custom-call(bf16[512,1024]{1,0:T(8,128)(2,1)} %bitcast.13, ...), custom_call_target="tpu_custom_call" | custom-call | flops 3221225472 | bytes 10485760 | tf_op jit(solution)/shard_map/window_project/pallas_call | solution.py:261
  3.3 2.5 %collective-permute-start = (bf16[80,1024]{1,0:T(8,128)(2,1)S(1)}, bf16[80,1024]{1,0:T(8,128)(2,1)S(1)}, u32[]{:S(2)}, u32[]{:S(2)}) collective-permute-start(bf16[80,1024]{1,0:T(8,128)(2,1)S(1)} %get-tuple-element.31), channel_id=1, source_target_pairs={{7,0},{0,1},{1,2},{2,3},{3,4},{4,5},{5,6},{6,7},{15,8},{8,9},{9,10... | collective-permute-start | bytes 491528 | tf_op jit(solution)/shard_map/ppermute | solution.py:442
  5.8 5.6 %window_inner.1 = (bf16[768,512]{1,0:T(8,128)(2,1)S(1)}, bf16[1024,1024]{1,0:T(8,128)(2,1)S(1)}, bf16[1024,1024]{1,0:T(8,128)(2,1)S(1)}, bf16[1024,1024]{1,0:T(8...) custom-call(f32[384,1024]{1,0:T(8,128)S(1)} %get-tuple-element.23.x_ref, ...), custom_call_target="tpu_custom_call" | custom-call | flops 3221225472 | bytes 10485760 | tf_op jit(solution)/shard_map/window_inner/pallas_call | solution.py:261
  11.5 1.4 %collective-permute-done.halo_ref = bf16[80,1024]{1,0:T(8,128)(2,1)S(1)} collective-permute-done((bf16[80,1024]{1,0:T(8,128)(2,1)S(1)}, bf16[80,1024]{1,0:T(8,128)(2,1)S(1)}, u32[]{:S(2)}, u32[]{:S(2)}) %collective-permute-start) | collective-permute-done | bytes 163872 | tf_op jit(solution)/shard_map/ppermute | solution.py:442
  12.9 2.2 %window_outer.1 = bf16[1024,512]{1,0:T(8,128)(2,1)S(1)} custom-call(bf16[768,512]{1,0:T(8,128)(2,1)S(1)} %get-tuple-element.30.inner_ref, bf16[80,1024]{1,0:T(8,128)(2,1)S(1)} %collective-permute-done.halo_ref, bf16[128,1024]{1,0:T(8,128)(2,1)S(1)} %get-tuple-element.32.edge_ref, f32[1,1024]{1,0:T(1,128)S(1)} %get-tuple-element.33.gain_ref, ...), custom_call_target="tpu_custom_call" | custom-call | flops 1073741824 | bytes 10485760 | tf_op jit(solution)/shard_map/window_outer/pallas_call | solution.py:261
  15.1 28.3 %all_to_all.10 = bf16[128,8,512]{2,1,0:T(8,128)(2,1)S(1)} all-to-all(bf16[128,8,512]{2,1,0:T(8,128)(2,1)S(1)} %bitcast.9), channel_id=1, replica_groups=mesh['lat'=16,'lon'=8] {'lat','lon'}, dimensions={0} | all-to-all | bytes 2097152 | tf_op jit(solution)/shard_map/all_to_all | solution.py:449
  43.4 6.8 %grid_part.1 = bf16[1024,512]{1,0:T(8,128)(2,1)S(1)} custom-call(bf16[1024,512]{1,0:T(8,128)(2,1)S(1)} %bitcast.11, s32[1,256]{1,0:T(1,128)S(1)} %get-tuple-element.28.pad_ref, f32[1,1024]{1,0:T(1,128)S(1)} %get-tuple-element.36.gain_ref, bf16[1024,1024]{1,0:T(8,128)(2,1)S(1)} %get-tuple-element.37.wq_ref, bf16[1024,1024]{1,0:T(8,128)(2,1)S(1)} %get-tuple-element.38.wk_ref, ...), custom_call_target="tpu_custom_call" | custom-call | flops 4294967296 | bytes 10485760 | tf_op jit(solution)/shard_map/grid_part/pallas_call | solution.py:261
  50.2 23.2 %all_to_all.11 = bf16[128,8,512]{2,1,0:T(8,128)(2,1)S(1)} all-to-all(bf16[128,8,512]{2,1,0:T(8,128)(2,1)S(1)} %bitcast.12), channel_id=1, replica_groups=mesh['lat'=16,'lon'=8] {'lat','lon'}, dimensions={0} | all-to-all | bytes 2097152 | tf_op jit(solution)/shard_map/all_to_all | solution.py:449
  73.5 1.1 %final_part.1 = bf16[512,1024]{1,0:T(8,128)(2,1)} custom-call(bf16[1024,512]{1,0:T(8,128)(2,1)S(1)} %bitcast.10), custom_call_target="tpu_custom_call" | custom-call | tf_op jit(solution)/shard_map/final_part/pallas_call | solution.py:428
Async XLA Ops:
  3.3 9.6 %collective-permute-start = (bf16[80,1024]{1,0:T(8,128)(2,1)S(1)}, bf16[80,1024]{1,0:T(8,128)(2,1)S(1)}, u32[]{:S(2)}, u32[]{:S(2)}) collective-permute-start(bf16[80,1024]{1,0:T(8,128)(2,1)S(1)} %get-tuple-element.31), channel_id=1, source_target_pairs={{7,0},{0,1},{1,2},{2,3},{3,4},{4,5},{5,6},{6,7},{15,8},{8,9},{9,10... | collective-permute-start | bytes 491528 | tf_op jit(solution)/shard_map/ppermute | solution.py:442

commit v6 on v4

--- a/solution.py
+++ b/solution.py
@@ -330,7 +330,7 @@
     pair = 2 * head_size
     chunks = wide_ref.shape[0]
     for chunk in range(chunks):
-        wide_ref[chunk] = block_ref[:, chunk * 128 : (chunk + 1) * 128].astype(F32)
+        wide_ref[chunk, : 2 * rows] = block_ref[:, chunk * 128 : (chunk + 1) * 128].astype(F32)
     lanes_of = [
         (slice(n * 128, (n + 1) * 128), n % chunks, n // chunks * groups)
         for n in range(2 * chunks)
@@ -377,7 +377,7 @@
         for lanes, chunk, start in lanes_of:
             wide_ref[chunk, pl.ds(start + group, members, stride=8), :] = home[:, lanes]
     for chunk in range(chunks):
-        out_ref[:, chunk * 128 : (chunk + 1) * 128] = wide_ref[chunk].astype(BF16)
+        out_ref[:, chunk * 128 : (chunk + 1) * 128] = wide_ref[chunk, : 2 * rows].astype(BF16)
 
 
 def grid_part(blocks, held):
@@ -389,7 +389,7 @@
         [blocks, *held],
         [],
         [
-            pltpu.VMEM((blocks.shape[1] // 128, blocks.shape[0], 128), F32),
+            pltpu.VMEM((blocks.shape[1] // 128, blocks.shape[0] + 8, 128), F32),
             pltpu.VMEM((rows, width), F32),
         ]
         + [pltpu.VMEM((rows, width), BF16)] * 5,

time: 74.1 us -> 74.1 us (level)
  no operation moved by 1% of the time
where the time goes in v6:
time: 74.1 us; the launch traced here: 74 us
  blocking collectives  50.8 us (69%)
  Pallas kernels  18.2 us (25%)
  starting transfers between devices  2.54 us (3%)
  waiting for transfers between devices  2.17 us (3%)
    all_to_all x2, blocking collectives, exchange(): lax.all_to_all(split, ('lat', 'lon'), split_axis=0, concat_axis=0, tiled=...  50.8 us
    pallas_call x4, Pallas kernels, call(): pl.pallas_call(kernel, out_shape=outs, in_specs=[VMEM_SPEC] * len(in_vmem...  17.2 us
    ppermute x1, starting transfers between devices, from_behind(): return lax.ppermute(block, axis, route)  2.54 us
    ppermute x1, waiting for transfers between devices, from_behind(): return lax.ppermute(block, axis, route)  2.17 us
  transfers between devices with their start and end apart: 1, of which 1 were waited for; matrix products, arithmetic and copies ran while one was open for 0% of the time, Pallas kernels for 7%

profile of v6, /device:TPU:1, one launch (start us, length us, event | category | flops | bytes accessed | tf_op | source)
XLA Modules:
  0.0 74.0 jit_solution(7801231352015554982)
XLA Ops:
  0.0 3.3 %window_project.1 = (bf16[80,1024]{1,0:T(8,128)(2,1)S(1)}, f32[384,1024]{1,0:T(8,128)S(1)}, bf16[128,1024]{1,0:T(8,128)(2,1)S(1)}, f32[8,1024]{1,0:T(8,128)S(1)}...) custom-call(bf16[512,1024]{1,0:T(8,128)(2,1)} %bitcast.13, ...), custom_call_target="tpu_custom_call" | custom-call | flops 3221225472 | bytes 10485760 | tf_op jit(solution)/shard_map/window_project/pallas_call | solution.py:254
  3.3 2.5 %collective-permute-start = (bf16[80,1024]{1,0:T(8,128)(2,1)S(1)}, bf16[80,1024]{1,0:T(8,128)(2,1)S(1)}, u32[]{:S(2)}, u32[]{:S(2)}) collective-permute-start(bf16[80,1024]{1,0:T(8,128)(2,1)S(1)} %get-tuple-element.31), channel_id=1, source_target_pairs={{7,0},{0,1},{1,2},{2,3},{3,4},{4,5},{5,6},{6,7},{15,8},{8,9},{9,10... | collective-permute-start | bytes 491528 | tf_op jit(solution)/shard_map/ppermute | solution.py:435
  5.8 4.9 %window_inner.1 = (bf16[768,512]{1,0:T(8,128)(2,1)S(1)}, bf16[1024,1024]{1,0:T(8,128)(2,1)S(1)}, bf16[1024,1024]{1,0:T(8,128)(2,1)S(1)}, bf16[1024,1024]{1,0:T(8...) custom-call(f32[384,1024]{1,0:T(8,128)S(1)} %get-tuple-element.23.x_ref, ...), custom_call_target="tpu_custom_call" | custom-call | flops 3221225472 | bytes 10485760 | tf_op jit(solution)/shard_map/window_inner/pallas_call | solution.py:254
  10.7 2.2 %collective-permute-done.halo_ref = bf16[80,1024]{1,0:T(8,128)(2,1)S(1)} collective-permute-done((bf16[80,1024]{1,0:T(8,128)(2,1)S(1)}, bf16[80,1024]{1,0:T(8,128)(2,1)S(1)}, u32[]{:S(2)}, u32[]{:S(2)}) %collective-permute-start) | collective-permute-done | bytes 163872 | tf_op jit(solution)/shard_map/ppermute | solution.py:435
  12.9 2.2 %window_outer.1 = bf16[1024,512]{1,0:T(8,128)(2,1)S(1)} custom-call(bf16[768,512]{1,0:T(8,128)(2,1)S(1)} %get-tuple-element.30.inner_ref, bf16[80,1024]{1,0:T(8,128)(2,1)S(1)} %collective-permute-done.halo_ref, bf16[128,1024]{1,0:T(8,128)(2,1)S(1)} %get-tuple-element.32.edge_ref, f32[1,1024]{1,0:T(1,128)S(1)} %get-tuple-element.33.gain_ref, ...), custom_call_target="tpu_custom_call" | custom-call | flops 1073741824 | bytes 10485760 | tf_op jit(solution)/shard_map/window_outer/pallas_call | solution.py:254
  15.1 27.6 %all_to_all.10 = bf16[128,8,512]{2,1,0:T(8,128)(2,1)S(1)} all-to-all(bf16[128,8,512]{2,1,0:T(8,128)(2,1)S(1)} %bitcast.9), channel_id=1, replica_groups=mesh['lat'=16,'lon'=8] {'lat','lon'}, dimensions={0} | all-to-all | bytes 2097152 | tf_op jit(solution)/shard_map/all_to_all | solution.py:442
  42.7 6.8 %grid_part.1 = bf16[1024,512]{1,0:T(8,128)(2,1)S(1)} custom-call(bf16[1024,512]{1,0:T(8,128)(2,1)S(1)} %bitcast.11, s32[1,256]{1,0:T(1,128)S(1)} %get-tuple-element.28.pad_ref, f32[1,1024]{1,0:T(1,128)S(1)} %get-tuple-element.36.gain_ref, bf16[1024,1024]{1,0:T(8,128)(2,1)S(1)} %get-tuple-element.37.wq_ref, bf16[1024,1024]{1,0:T(8,128)(2,1)S(1)} %get-tuple-element.38.wk_ref, ...), custom_call_target="tpu_custom_call" | custom-call | flops 4294967296 | bytes 10485760 | tf_op jit(solution)/shard_map/grid_part/pallas_call | solution.py:254
  49.5 23.3 %all_to_all.11 = bf16[128,8,512]{2,1,0:T(8,128)(2,1)S(1)} all-to-all(bf16[128,8,512]{2,1,0:T(8,128)(2,1)S(1)} %bitcast.12), channel_id=1, replica_groups=mesh['lat'=16,'lon'=8] {'lat','lon'}, dimensions={0} | all-to-all | bytes 2097152 | tf_op jit(solution)/shard_map/all_to_all | solution.py:442
  72.8 1.1 %final_part.1 = bf16[512,1024]{1,0:T(8,128)(2,1)} custom-call(bf16[1024,512]{1,0:T(8,128)(2,1)S(1)} %bitcast.10), custom_call_target="tpu_custom_call" | custom-call | tf_op jit(solution)/shard_map/final_part/pallas_call | solution.py:421
Async XLA Ops:
  3.3 9.6 %collective-permute-start = (bf16[80,1024]{1,0:T(8,128)(2,1)S(1)}, bf16[80,1024]{1,0:T(8,128)(2,1)S(1)}, u32[]{:S(2)}, u32[]{:S(2)}) collective-permute-start(bf16[80,1024]{1,0:T(8,128)(2,1)S(1)} %get-tuple-element.31), channel_id=1, source_target_pairs={{7,0},{0,1},{1,2},{2,3},{3,4},{4,5},{5,6},{6,7},{15,8},{8,9},{9,10... | collective-permute-start | bytes 491528 | tf_op jit(solution)/shard_map/ppermute | solution.py:435

commit v7 on v5

--- a/solution.py
+++ b/solution.py
@@ -108,7 +108,8 @@
         return jnp.concatenate(exps, axis=1)
 
     units = [(tile, group) for group in range(GROUPS) for tile in range(len(bands))]
-    batches = [units[at : at + 4] for at in range(0, len(units), 4)]
+    size = min(8, len(units))
+    batches = [units[at : at + size] for at in range(0, len(units), size)]
 
     def finish(batch, weights):
         totals = matmul(jnp.concatenate(weights, axis=0), ones)

time: 74.8 us -> 73.9 us (0.988)
  Pallas kernels: 19 us -> 18 us
  waiting for transfers between devices: 1.41 us -> 2.33 us
  blocking collectives: 51.6 us -> 50.7 us
    pallas_call x4, Pallas kernels: 17.9 us -> 17 us  [call(): pl.pallas_call(kernel, out_shape=outs, in_specs=[VMEM_SPEC] * len(in_vmem...]
    ppermute x1, waiting for transfers between devices: 1.41 us -> 2.33 us  [from_behind(): return lax.ppermute(block, axis, route)]
    all_to_all x2, blocking collectives: 51.6 us -> 50.7 us  [exchange(): lax.all_to_all(split, ('lat', 'lon'), split_axis=0, concat_axis=0, tiled=...]
  transfers between devices with their start and end apart: 1 -> 1, of which waited for: 1 -> 1; matrix products, arithmetic and copies ran while one was open for 0% -> 0% of each run, Pallas kernels for 8% -> 6%
where the time goes in v7:
time: 73.9 us; the launch traced here: 73.8 us
  blocking collectives  50.7 us (69%)
  Pallas kernels  18 us (24%)
  starting transfers between devices  2.54 us (3%)
  waiting for transfers between devices  2.33 us (3%)
    all_to_all x2, blocking collectives, exchange(): lax.all_to_all(split, ('lat', 'lon'), split_axis=0, concat_axis=0, tiled=...  50.7 us
    pallas_call x4, Pallas kernels, call(): pl.pallas_call(kernel, out_shape=outs, in_specs=[VMEM_SPEC] * len(in_vmem...  17 us
    ppermute x1, starting transfers between devices, from_behind(): return lax.ppermute(block, axis, route)  2.54 us
    ppermute x1, waiting for transfers between devices, from_behind(): return lax.ppermute(block, axis, route)  2.33 us
  transfers between devices with their start and end apart: 1, of which 1 were waited for; matrix products, arithmetic and copies ran while one was open for 0% of the time, Pallas kernels for 6%

profile of v7, /device:TPU:1, one launch (start us, length us, event | category | flops | bytes accessed | tf_op | source)
XLA Modules:
  0.0 73.8 jit_solution(5578548656325883491)
XLA Ops:
  0.0 3.3 %window_project.1 = (bf16[80,1024]{1,0:T(8,128)(2,1)S(1)}, f32[384,1024]{1,0:T(8,128)S(1)}, bf16[128,1024]{1,0:T(8,128)(2,1)S(1)}, f32[8,1024]{1,0:T(8,128)S(1)}...) custom-call(bf16[512,1024]{1,0:T(8,128)(2,1)} %bitcast.13, ...), custom_call_target="tpu_custom_call" | custom-call | flops 3221225472 | bytes 10485760 | tf_op jit(solution)/shard_map/window_project/pallas_call | solution.py:262
  3.3 2.5 %collective-permute-start = (bf16[80,1024]{1,0:T(8,128)(2,1)S(1)}, bf16[80,1024]{1,0:T(8,128)(2,1)S(1)}, u32[]{:S(2)}, u32[]{:S(2)}) collective-permute-start(bf16[80,1024]{1,0:T(8,128)(2,1)S(1)} %get-tuple-element.31), channel_id=1, source_target_pairs={{7,0},{0,1},{1,2},{2,3},{3,4},{4,5},{5,6},{6,7},{15,8},{8,9},{9,10... | collective-permute-start | bytes 491528 | tf_op jit(solution)/shard_map/ppermute | solution.py:443
  5.8 4.7 %window_inner.1 = (bf16[768,512]{1,0:T(8,128)(2,1)S(1)}, bf16[1024,1024]{1,0:T(8,128)(2,1)S(1)}, bf16[1024,1024]{1,0:T(8,128)(2,1)S(1)}, bf16[1024,1024]{1,0:T(8...) custom-call(f32[384,1024]{1,0:T(8,128)S(1)} %get-tuple-element.23.x_ref, ...), custom_call_target="tpu_custom_call" | custom-call | flops 3221225472 | bytes 10485760 | tf_op jit(solution)/shard_map/window_inner/pallas_call | solution.py:262
  10.6 2.3 %collective-permute-done.halo_ref = bf16[80,1024]{1,0:T(8,128)(2,1)S(1)} collective-permute-done((bf16[80,1024]{1,0:T(8,128)(2,1)S(1)}, bf16[80,1024]{1,0:T(8,128)(2,1)S(1)}, u32[]{:S(2)}, u32[]{:S(2)}) %collective-permute-start) | collective-permute-done | bytes 163872 | tf_op jit(solution)/shard_map/ppermute | solution.py:443
  12.9 2.2 %window_outer.1 = bf16[1024,512]{1,0:T(8,128)(2,1)S(1)} custom-call(bf16[768,512]{1,0:T(8,128)(2,1)S(1)} %get-tuple-element.30.inner_ref, bf16[80,1024]{1,0:T(8,128)(2,1)S(1)} %collective-permute-done.halo_ref, bf16[128,1024]{1,0:T(8,128)(2,1)S(1)} %get-tuple-element.32.edge_ref, f32[1,1024]{1,0:T(1,128)S(1)} %get-tuple-element.33.gain_ref, ...), custom_call_target="tpu_custom_call" | custom-call | flops 1073741824 | bytes 10485760 | tf_op jit(solution)/shard_map/window_outer/pallas_call | solution.py:262
  15.1 27.4 %all_to_all.10 = bf16[128,8,512]{2,1,0:T(8,128)(2,1)S(1)} all-to-all(bf16[128,8,512]{2,1,0:T(8,128)(2,1)S(1)} %bitcast.9), channel_id=1, replica_groups=mesh['lat'=16,'lon'=8] {'lat','lon'}, dimensions={0} | all-to-all | bytes 2097152 | tf_op jit(solution)/shard_map/all_to_all | solution.py:450
  42.5 6.8 %grid_part.1 = bf16[1024,512]{1,0:T(8,128)(2,1)S(1)} custom-call(bf16[1024,512]{1,0:T(8,128)(2,1)S(1)} %bitcast.11, s32[1,256]{1,0:T(1,128)S(1)} %get-tuple-element.28.pad_ref, f32[1,1024]{1,0:T(1,128)S(1)} %get-tuple-element.36.gain_ref, bf16[1024,1024]{1,0:T(8,128)(2,1)S(1)} %get-tuple-element.37.wq_ref, bf16[1024,1024]{1,0:T(8,128)(2,1)S(1)} %get-tuple-element.38.wk_ref, ...), custom_call_target="tpu_custom_call" | custom-call | flops 4294967296 | bytes 10485760 | tf_op jit(solution)/shard_map/grid_part/pallas_call | solution.py:262
  49.3 23.3 %all_to_all.11 = bf16[128,8,512]{2,1,0:T(8,128)(2,1)S(1)} all-to-all(bf16[128,8,512]{2,1,0:T(8,128)(2,1)S(1)} %bitcast.12), channel_id=1, replica_groups=mesh['lat'=16,'lon'=8] {'lat','lon'}, dimensions={0} | all-to-all | bytes 2097152 | tf_op jit(solution)/shard_map/all_to_all | solution.py:450
  72.6 1.1 %final_part.1 = bf16[512,1024]{1,0:T(8,128)(2,1)} custom-call(bf16[1024,512]{1,0:T(8,128)(2,1)S(1)} %bitcast.10), custom_call_target="tpu_custom_call" | custom-call | tf_op jit(solution)/shard_map/final_part/pallas_call | solution.py:429
Async XLA Ops:
  3.3 9.6 %collective-permute-start = (bf16[80,1024]{1,0:T(8,128)(2,1)S(1)}, bf16[80,1024]{1,0:T(8,128)(2,1)S(1)}, u32[]{:S(2)}, u32[]{:S(2)}) collective-permute-start(bf16[80,1024]{1,0:T(8,128)(2,1)S(1)} %get-tuple-element.31), channel_id=1, source_target_pairs={{7,0},{0,1},{1,2},{2,3},{3,4},{4,5},{5,6},{6,7},{15,8},{8,9},{9,10... | collective-permute-start | bytes 491528 | tf_op jit(solution)/shard_map/ppermute | solution.py:443
